TPU v7x, 32 devices: a whole 2x2x4 slice. The times are simulated.
32 devices in a mesh: grp: 2 (over x), store: 16 (over z, y, core).
Axes of the slice: x: 2, y: 2, z: 4, core: 2. Of those that a mesh axis runs over, the one named last changes fastest.
Arguments:
- query_inputs: bfloat16 [128, 16, 4096], P(('grp', 'store')), parts along dimension 0, may hold values from -6 to 6
- query_grads: bfloat16 [128, 16, 4096], P(('grp', 'store')), parts along dimension 0, may hold values from -0.099609375 to 0.099609375
- hash_in: int32 [4096], replicated, may hold values from 0 to 4095
- sign_in: int32 [4096], replicated, may hold values from 0 to 1
- hash_out: int32 [4096], replicated, may hold values from 0 to 4095
- sign_out: int32 [4096], replicated, may hold values from 0 to 1
- stored: bfloat16 [128, 4096], P(('grp', 'store')), parts along dimension 0, may hold values from -0.099609375 to 0.099609375
Outputs:
- scores: float32 [128, 64], P(('grp', 'store')), parts along dimension 0
- influence: float32 [128], P(('grp', 'store')), parts along dimension 0
There are 2 independent parts, one for each index of `grp`. A program takes and returns all parts, laid end to end along the dimension named above; an argument that names none is the same for every part. Nothing has to cross between parts.
All inputs are finite; a program needn't handle non-finite values.
Results may differ from a plain program's by a relative error of at most 0.0029.
Values may be sent and summed in bfloat16 or wider, within the bound.
No kernel may reach another device: no remote copies, remote signals or barrier semaphores. Data moves between devices by JAX's collectives and lax.ppermute only.
A program may use at most 64 MiB of HBM per device.

v0:
```python
import functools, math
import numpy as np
import jax, jax.numpy as jnp
from jax import lax
from jax.experimental import pallas as pl
from jax.experimental.pallas import tpu as pltpu
from jax.sharding import PartitionSpec as P

bf = jnp.bfloat16
f32 = jnp.float32
NT = (((1,), (1,)), ((), ()))
VMEM_LIMIT = 60 << 20
RADIX = 16


def rfft(x):
    n=len(x)
    if n==1: return [(x[0],None)]
    if n==2: return [(x[0]+x[1],None),(x[0]-x[1],None)]
    e=rfft(x[0::2]); o=rfft(x[1::2]); h=n//2; out=[None]*(h+1)
    out[0]=(e[0][0]+o[0][0],None); out[h]=(e[0][0]-o[0][0],None)
    for k in range(1,h//2):
        c,s=math.cos(2*math.pi*k/n),math.sin(2*math.pi*k/n)
        re,im=o[k]
        if 8*k==n:
            tr=(re+im)*c; ti=(im-re)*c
        else:
            tr=re*c+im*s; ti=im*c-re*s
        out[k]=(e[k][0]+tr,e[k][1]+ti); out[h-k]=(e[k][0]-tr,ti-e[k][1])
    out[h//2]=(e[h//2][0],-o[h//2][0])
    return out

def irfft(X):
    h=len(X)-1; n=2*h
    if h==0: return [X[0][0]]
    if h==1: return [X[0][0]+X[1][0],X[0][0]-X[1][0]]
    E=[None]*(h//2+1); O=[None]*(h//2+1)
    E[0]=(X[0][0]+X[h][0],None); O[0]=(X[0][0]-X[h][0],None)
    for k in range(1,h//2):
        c,s=math.cos(2*math.pi*k/n),math.sin(2*math.pi*k/n)
        (ar,ai),(br,bi)=X[k],X[h-k]
        E[k]=(ar+br,ai-bi)
        dr,di=ar-br,ai+bi
        if 8*k==n: O[k]=((dr-di)*c,(dr+di)*c)
        else: O[k]=(dr*c-di*s,dr*s+di*c)
    r,i=X[h//2]
    E[h//2]=(2.0*r,None); O[h//2]=(-2.0*i,None)
    ev=irfft(E); od=irfft(O); out=[None]*n
    out[0::2]=ev; out[1::2]=od
    return out


def tables(A, W):
    i = np.arange(W)
    ang = 2 * np.pi * (np.outer(i, i) % W) / W
    c, s = np.cos(ang), np.sin(ang)
    m = np.block([[c, -s], [s, c]]).astype(np.float32)
    hi = m.astype(jnp.bfloat16)
    lo = (m - hi.astype(np.float32)).astype(jnp.bfloat16)
    t = 2 * np.pi * np.outer(np.arange(A // 2 + 1), i) / (A * W)
    tw = np.concatenate([np.cos(t), np.sin(t)], 0).astype(np.float32)
    tw = np.concatenate([tw, np.zeros((-len(tw) % 8, W), np.float32)], 0)
    return np.concatenate([hi, lo], 0), tw


def split(z):
    hi = z.astype(bf)
    return hi, (z - hi.astype(f32)).astype(bf)


def onehot(h_ref, bt, W):
    it = lax.broadcasted_iota(jnp.int32, (W, 128), 0).astype(f32).astype(bf)
    one, zero = jnp.ones((W, 128), bf), jnp.zeros((W, 128), bf)
    for j in range(h_ref.shape[0]):
        b = (h_ref[j : j + 1, :] & (W - 1)).astype(f32).astype(bf)
        bt[:, j * 128 : (j + 1) * 128] = jnp.where(it == jnp.broadcast_to(b, (W, 128)), one, zero)


def count(x, h_ref, s_ref, bt, A, W):
    cols = []
    for j in range(h_ref.shape[0]):
        sg = (2 * s_ref[j : j + 1, :] - 1).astype(f32).astype(bf)
        a = lax.shift_right_logical(h_ref[j : j + 1, :], W.bit_length() - 1).astype(f32).astype(bf)
        xs = x[:, j * 128 : (j + 1) * 128] * sg
        ab = jnp.broadcast_to(a, xs.shape)
        z = jnp.zeros_like(xs)
        cols.append(jnp.concatenate([jnp.where(ab == jnp.asarray(k, bf), xs, z) for k in range(A)], 0))
    return lax.dot_general(jnp.concatenate(cols, 1), bt[...], NT, preferred_element_type=f32)


def class_rows(cnt, q, T, tw, z, row0, A, W):
    H = A // 2 + 1
    for t in range(0, T, 8):
        for l in range(0, W, 128):
            planes = [cnt[k, pl.ds(pl.multiple_of(q * T + t, 8), 8), l : l + 128] for k in range(A)]
            for n, (re, im) in enumerate(rfft(planes)):
                if n:
                    c, s = tw[n : n + 1, l : l + 128], tw[H + n : H + n + 1, l : l + 128]
                    re, im = (re * c, -re * s) if im is None else (re * c + im * s, im * c - re * s)
                else:
                    im = jnp.zeros_like(re)
                r = slice(row0 + n * T + t, row0 + n * T + t + 8)
                z[r, l : l + 128] = re
                z[r, W + l : W + l + 128] = im


def dft(z, m, W):
    hi, lo = split(z)
    lhs = jnp.concatenate([hi, lo, hi], 1)
    out = []
    for o in (0, W):
        m_hi, m_lo = m[: 2 * W, o : o + W], m[2 * W :, o : o + W]
        out.append(jnp.dot(lhs, jnp.concatenate([m_hi, m_hi, m_lo], 0), preferred_element_type=f32))
    return out


def kernel(x_hbm, y_hbm, hi_hbm, si_hbm, ho_hbm, so_hbm, m_hbm, tw_hbm, o_ref,
           x, h, s, m, tw, bt, cnt, za, zb, p, sem, *, Q, T, A, W):
    H, R = A // 2 + 1, Q * T
    for i, pairs in enumerate((((hi_hbm, h), (si_hbm, s), (x_hbm, x)), ((ho_hbm, h), (so_hbm, s), (y_hbm, x)))):
        for j, (a, b) in enumerate(pairs):
            pltpu.make_async_copy(a, b.at[i], sem.at[i, j]).start()
    tables_in = [pltpu.make_async_copy(tw_hbm, tw, sem.at[2, 0]), pltpu.make_async_copy(m_hbm, m, sem.at[2, 1])]
    for c in tables_in:
        c.start()
    p[...] = jnp.zeros_like(p)

    def counts(i, carry):
        for j, (a, b) in enumerate(((hi_hbm, h), (si_hbm, s), (x_hbm, x))):
            pltpu.make_async_copy(a, b.at[i], sem.at[i, j]).wait()
        onehot(h.at[i], bt, W)
        cnt[i] = count(x.at[i], h.at[i], s.at[i], bt, A, W).reshape(A, R, W)
        return carry

    lax.fori_loop(0, 2, counts, 0)
    for c in tables_in:
        c.wait()

    def rows(q, z):
        for i in range(2):
            class_rows(cnt.at[i], q, T, tw, z, i * H * T, A, W)

    def product(q, z):
        re, im = dft(z[...], m, W)
        here = lax.broadcasted_iota(jnp.int32, (8, W), 0) == q
        for k in range(H):
            a, b = slice(k * T, (k + 1) * T), slice((H + k) * T, (H + k + 1) * T)
            pr = jnp.sum(re[a] * re[b] - im[a] * im[b], 0, keepdims=True)
            pi = jnp.sum(re[a] * im[b] + im[a] * re[b], 0, keepdims=True)
            r = slice(8 * k, 8 * k + 8)
            p[r, :W] = jnp.where(here, jnp.broadcast_to(pr, (8, W)), p[r, :W])
            p[r, W:] = jnp.where(here, jnp.broadcast_to(pi, (8, W)), p[r, W:])

    rows(0, za)

    def two(j, carry):
        rows(2 * j + 1, zb)
        product(2 * j, za)
        rows(jnp.minimum(2 * j + 2, Q - 1), za)
        product(2 * j + 1, zb)
        return carry

    lax.fori_loop(0, Q // 2, two, 0)
    for k, v in enumerate(back(p[...], m, tw, A, W)):
        o_ref[:, k * W : (k + 1) * W] = v[:Q].astype(o_ref.dtype)


def back(p, m, tw, A, W):
    H = A // 2 + 1
    scale = 1.0 / (A * W)
    re_all, im_all = dft(p * jnp.where(lax.broadcasted_iota(jnp.int32, p.shape, 1) < W, scale, -scale), m, W)
    X = []
    for k in range(H):
        re, im = re_all[8 * k : 8 * k + 8], -im_all[8 * k : 8 * k + 8]
        if k == 0:
            X.append((re, None))
            continue
        c, s = tw[k : k + 1, :], tw[H + k : H + k + 1, :]
        X.append((re * c - im * s, None if k == A // 2 else re * s + im * c))
    return irfft(X)


def sketch(x, y, hash_in, sign_in, hash_out, sign_out, width):
    Q, T, D = x.shape
    assert Q <= 8 and Q % 2 == 0 and y.shape[2] == D
    A, W = RADIX, width // RADIX
    H, R = A // 2 + 1, Q * T
    m, tw = (jnp.asarray(v) for v in tables(A, W))
    hs = [v.reshape(-1, 128) for v in (hash_in, sign_in, hash_out, sign_out)]
    x, y = x.reshape(R, D), y.reshape(R, -1)
    any_ = pl.BlockSpec(memory_space=pl.ANY)
    return pl.pallas_call(
        functools.partial(kernel, Q=Q, T=T, A=A, W=W),
        out_shape=jax.ShapeDtypeStruct((Q, width), bf),
        in_specs=[any_] * 8,
        out_specs=pl.BlockSpec(memory_space=pltpu.VMEM),
        scratch_shapes=[
            pltpu.VMEM((2, R, D), bf), pltpu.VMEM((2, D // 128, 128), jnp.int32), pltpu.VMEM((2, D // 128, 128), jnp.int32),
            pltpu.VMEM(m.shape, bf), pltpu.VMEM(tw.shape, f32),
            pltpu.VMEM((W, D), bf), pltpu.VMEM((2, A, R, W), f32), pltpu.VMEM((2 * H * T, 2 * W), f32), pltpu.VMEM((2 * H * T, 2 * W), f32),
            pltpu.VMEM((H * 8, 2 * W), f32), pltpu.SemaphoreType.DMA((3, 3)),
        ],
        cost_estimate=pl.CostEstimate(flops=4 * R * D * width, bytes_accessed=4 << 20, transcendentals=0),
        compiler_params=pltpu.CompilerParams(vmem_limit_bytes=VMEM_LIMIT),
    )(x, y, *hs, m, tw)


def score_kernel(me_ref, sk_ref, near_ref, far_ref, s_ref, t_ref, *, bits, e):
    q = sk_ref.shape[0]
    rows = jnp.concatenate([near_ref[...], far_ref[...]], 0)
    s = lax.dot_general(sk_ref[...], rows, NT, preferred_element_type=f32)
    t_ref[...] = jnp.sum(s, 0, keepdims=True)
    count = rows.shape[0]
    p = lax.broadcasted_iota(jnp.int32, (count, count), 0)
    shift = e.bit_length() - 1
    device = jnp.broadcast_to(me_ref[0], p.shape)
    for i, bit in enumerate(bits):
        device = device ^ (((p >> (shift + i)) & 1) * bit)
    place = (device << shift) | (p & (e - 1))
    move = jnp.where(place == lax.broadcasted_iota(jnp.int32, p.shape, 1), 1.0, 0.0).astype(bf)
    hi = s.astype(bf)
    rest = s - hi.astype(f32)
    mid = rest.astype(bf)
    low = (rest - mid.astype(f32)).astype(bf)
    moved = [jnp.dot(v, move, preferred_element_type=f32) for v in (hi, mid, low)]
    s_ref[...] = moved[0] + (moved[1] + moved[2])


def score(me, sk, near, far, bits):
    q, e = sk.shape[0], near.shape[0] * 2 >> len(bits)
    total = near.shape[0] * 2
    assert e & (e - 1) == 0
    vm = pl.BlockSpec(memory_space=pltpu.VMEM)
    return pl.pallas_call(
        functools.partial(score_kernel, bits=bits, e=e),
        out_shape=(jax.ShapeDtypeStruct((q, total), f32), jax.ShapeDtypeStruct((1, total), f32)),
        in_specs=[pl.BlockSpec(memory_space=pltpu.SMEM), vm, vm, vm],
        out_specs=(vm, vm),
        cost_estimate=pl.CostEstimate(flops=2 * q * total * sk.shape[1], bytes_accessed=near.size * 4, transcendentals=0),
        compiler_params=pltpu.CompilerParams(vmem_limit_bytes=16 << 20),
    )(me.reshape(1), sk, near, far)


def swap(v, bit, n):
    return lax.ppermute(v, "store", [(i, i ^ bit) for i in range(n)])


def body(query_inputs, query_grads, hash_in, sign_in, hash_out, sign_out, stored):
    n = lax.axis_size("store")
    q_dev, e = query_inputs.shape[0], stored.shape[0]
    bits = [1 << b for b in reversed(range(n.bit_length() - 1))]
    rows = stored
    for bit in bits[:-2]:
        rows = jnp.concatenate([rows, swap(rows, bit, n)], 0)
    rows, hash_in = lax.optimization_barrier((rows, hash_in))
    other = swap(rows, bits[-2], n)
    sk = sketch(query_inputs, query_grads, hash_in, sign_in, hash_out, sign_out, stored.shape[1])
    rows = jnp.concatenate([rows, other], 0)
    scores, t = score(lax.axis_index("store"), sk, rows, swap(rows, bits[-1], n), bits)
    t = t.reshape(-1)
    for bit in reversed(bits):
        half = t.shape[0] // 2
        t = t[:half] + swap(t[half:], bit, n)
    return scores, t / (n * q_dev)


def solution(mesh):
    rows = P(("grp", "store"), None)
    cube = P(("grp", "store"), None, None)
    return jax.shard_map(
        body,
        mesh=mesh,
        in_specs=(cube, cube, P(), P(), P(), P(), rows),
        out_specs=(rows, P(("grp", "store"))),
        check_vma=False,
    )
```

profile of v0, /device:TPU:0, one launch (start us, length us, event | category | flops | bytes accessed | tf_op | source)
XLA Modules:
  0.0 43.1 jit_solution(5664444956994827936)
XLA Ops:
  0.6 0.0 copy-start.1
  0.6 4.1 %collective-permute-start = (bf16[4,4096]{1,0:T(4,128)(2,1)}, bf16[4,4096]{1,0:T(4,128)(2,1)S(1)}, u32[]{:S(2)}, u32[]{:S(2)}) collective-permute-start(bf16[4,4096]{1,0:T(4,128)(2,1)} %param.15), channel_id=1, source_target_pairs={{0,8},{1,9},{2,10},{3,11},{4,12},{5,13},{6,14},{7,15},{8,0},{9,1},... | collective-permute-start | bytes 98312 | tf_op jit(solution)/shard_map/ppermute | solution.py:245
  4.7 2.5 %collective-permute-done = bf16[4,4096]{1,0:T(4,128)(2,1)S(1)} collective-permute-done((bf16[4,4096]{1,0:T(4,128)(2,1)}, bf16[4,4096]{1,0:T(4,128)(2,1)S(1)}, u32[]{:S(2)}, u32[]{:S(2)}) %collective-permute-start) | collective-permute-done | bytes 32800 | tf_op jit(solution)/shard_map/ppermute | solution.py:245
  7.2 0.8 %pad_maximum_fusion.1 = bf16[8,4096]{1,0:T(8,128)(2,1)S(1)} fusion(bf16[4,4096]{1,0:T(4,128)(2,1)S(1)} %collective-permute-done, bf16[4,4096]{1,0:T(4,128)(2,1)} %param.15), kind=kLoop, calls=%fused_computation.1 | loop fusion | flops 131072 | bytes 131072 | tf_op jit(solution)/shard_map/concatenate | solution.py:254
  8.0 1.6 %collective-permute-start.1 = (bf16[8,4096]{1,0:T(8,128)(2,1)S(1)}, bf16[8,4096]{1,0:T(8,128)(2,1)S(1)}, u32[]{:S(2)}, u32[]{:S(2)}) collective-permute-start(bf16[8,4096]{1,0:T(8,128)(2,1)S(1)} %pad_maximum_fusion.1), channel_id=1, source_target_pairs={{0,4},{1,5},{2,6},{3,7},{4,0},{5,1},{6,2},{7,3},{8,12},{9,13},{10,... | collective-permute-start | bytes 196616 | tf_op jit(solution)/shard_map/ppermute | solution.py:245
  9.6 2.7 %collective-permute-done.1 = bf16[8,4096]{1,0:T(8,128)(2,1)S(1)} collective-permute-done((bf16[8,4096]{1,0:T(8,128)(2,1)S(1)}, bf16[8,4096]{1,0:T(8,128)(2,1)S(1)}, u32[]{:S(2)}, u32[]{:S(2)}) %collective-permute-start.1) | collective-permute-done | bytes 65568 | tf_op jit(solution)/shard_map/ppermute | solution.py:245
  12.3 0.0 copy-done.1
  12.3 0.1 pad_maximum_fusion
  12.4 1.8 %collective-permute-start.2 = (bf16[16,4096]{1,0:T(8,128)(2,1)S(1)}, bf16[16,4096]{1,0:T(8,128)(2,1)S(1)}, u32[]{:S(2)}, u32[]{:S(2)}) collective-permute-start(bf16[16,4096]{1,0:T(8,128)(2,1)S(1)} %pad_maximum_fusion), channel_id=1, source_target_pairs={{0,2},{1,3},{2,0},{3,1},{4,6},{5,7},{6,4},{7,5},{8,10},{9,11},{10,... | collective-permute-start | bytes 393224 | tf_op jit(solution)/shard_map/ppermute | solution.py:245
  14.2 3.2 %collective-permute-done.2 = bf16[16,4096]{1,0:T(8,128)(2,1)S(1)} collective-permute-done((bf16[16,4096]{1,0:T(8,128)(2,1)S(1)}, bf16[16,4096]{1,0:T(8,128)(2,1)S(1)}, u32[]{:S(2)}, u32[]{:S(2)}) %collective-permute-start.2) | collective-permute-done | bytes 131104 | tf_op jit(solution)/shard_map/ppermute | solution.py:245
  17.4 0.1 collective-permute-start.3
  17.5 10.2 %shard_map.104.sk_ref = bf16[4,4096]{1,0:T(4,128)(2,1)} custom-call(bf16[64,4096]{1,0:T(8,128)(2,1)} %bitcast.11, bf16[64,4096]{1,0:T(8,128)(2,1)} %bitcast.12, s32[32,128]{1,0:T(8,128)} %bitcast.13, s32[32,128]{1,0:T(8,128)} %bitcast.14, s32[32,128]{1,0:T(8,128)} %bitcast.15, s32[32,128]{1,0:T(8,128)} %bitcast.16, bf16[1024,512]{1,0:T(8,128)(2,1)} %constant.11.clone.m_hbm, ...), custom_call_target="tpu_custom_call" | custom-call | flops 4294967296 | bytes 4194304 | tf_op jit(solution)/shard_map/pallas_call | solution.py:192
  27.7 0.0 collective-permute-done.3.far_ref
  27.7 0.0 copy-start
  27.7 0.7 %copy-done = bf16[4,4096]{1,0:T(4,128)(2,1)S(1)} copy-done((bf16[4,4096]{1,0:T(4,128)(2,1)S(1)}, bf16[4,4096]{1,0:T(4,128)(2,1)}, u32[]{:S(2)}) %copy-start) | copy-done | bytes 32792
  28.5 1.0 %shard_map.105 = (f32[4,64]{1,0:T(4,128)}, f32[1,64]{1,0:T(1,128)S(1)}) custom-call(s32[1]{0:T(128)} %bitcast.me_ref, bf16[4,4096]{1,0:T(4,128)(2,1)S(1)} %copy-done, bf16[32,4096]{1,0:T(8,128)(2,1)S(1)} %constant_dynamic-update-slice_fusion.near_ref, bf16[32,4096]{1,0:T(8,128)(2,1)S(1)} %collective-permute-done.3.far_ref), custom_call_target="tpu_custom_call" | custom-call | flops 2097152 | bytes 524288 | tf_op jit(solution)/shard_map/pallas_call | solution.py:234
  29.5 0.1 slice_bitcast_fusion
  29.5 0.5 %collective-permute-start.4 = (f32[32]{0:T(128)S(1)}, f32[32]{0:T(128)S(1)}, u32[]{:S(2)}, u32[]{:S(2)}) collective-permute-start(f32[32]{0:T(128)S(1)} %slice_bitcast_fusion), channel_id=1, source_target_pairs={{0,1},{1,0},{2,3},{3,2},{4,5},{5,4},{6,7},{7,6},{8,9},{9,8},{10,11... | collective-permute-start | bytes 392 | tf_op jit(solution)/shard_map/ppermute | solution.py:245
  30.0 0.8 %collective-permute-done.4 = f32[32]{0:T(128)S(1)} collective-permute-done((f32[32]{0:T(128)S(1)}, f32[32]{0:T(128)S(1)}, u32[]{:S(2)}, u32[]{:S(2)}) %collective-permute-start.4) | collective-permute-done | bytes 160 | tf_op jit(solution)/shard_map/ppermute | solution.py:245
  30.9 0.1 slice.35
  30.9 1.7 %collective-permute-start.5 = (f32[16]{0:T(128)S(1)}, f32[16]{0:T(128)S(1)}, u32[]{:S(2)}, u32[]{:S(2)}) collective-permute-start(f32[16]{0:T(128)S(1)} %slice.35), channel_id=1, source_target_pairs={{0,2},{1,3},{2,0},{3,1},{4,6},{5,7},{6,4},{7,5},{8,10},{9,11},{10,... | collective-permute-start | bytes 200 | tf_op jit(solution)/shard_map/ppermute | solution.py:245
  32.7 1.8 %collective-permute-done.5 = f32[16]{0:T(128)S(1)} collective-permute-done((f32[16]{0:T(128)S(1)}, f32[16]{0:T(128)S(1)}, u32[]{:S(2)}, u32[]{:S(2)}) %collective-permute-start.5) | collective-permute-done | bytes 96 | tf_op jit(solution)/shard_map/ppermute | solution.py:245
  34.5 0.1 slice.37
  34.6 1.6 %collective-permute-start.6 = (f32[8]{0:T(128)S(1)}, f32[8]{0:T(128)S(1)}, u32[]{:S(2)}, u32[]{:S(2)}) collective-permute-start(f32[8]{0:T(128)S(1)} %slice.37), channel_id=1, source_target_pairs={{0,4},{1,5},{2,6},{3,7},{4,0},{5,1},{6,2},{7,3},{8,12},{9,13},{10,... | collective-permute-start | bytes 104 | tf_op jit(solution)/shard_map/ppermute | solution.py:245
  36.1 2.0 %collective-permute-done.6 = f32[8]{0:T(128)S(1)} collective-permute-done((f32[8]{0:T(128)S(1)}, f32[8]{0:T(128)S(1)}, u32[]{:S(2)}, u32[]{:S(2)}) %collective-permute-start.6) | collective-permute-done | bytes 64 | tf_op jit(solution)/shard_map/ppermute | solution.py:245
  38.1 0.1 slice.39
  38.2 2.6 %collective-permute-start.7 = (f32[4]{0:T(128)S(1)}, f32[4]{0:T(128)S(1)}, u32[]{:S(2)}, u32[]{:S(2)}) collective-permute-start(f32[4]{0:T(128)S(1)} %slice.39), channel_id=1, source_target_pairs={{0,8},{1,9},{2,10},{3,11},{4,12},{5,13},{6,14},{7,15},{8,0},{9,1},... | collective-permute-start | bytes 56 | tf_op jit(solution)/shard_map/ppermute | solution.py:245
  40.8 1.8 %collective-permute-done.7 = f32[4]{0:T(128)S(1)} collective-permute-done((f32[4]{0:T(128)S(1)}, f32[4]{0:T(128)S(1)}, u32[]{:S(2)}, u32[]{:S(2)}) %collective-permute-start.7) | collective-permute-done | bytes 48 | tf_op jit(solution)/shard_map/ppermute | solution.py:245
  42.6 0.5 %add_multiply_fusion = f32[4]{0:T(128)} fusion(f32[4]{0:T(128)S(1)} %collective-permute-done.7, f32[8]{0:T(128)S(1)} %slice_add_fusion), kind=kLoop, calls=%fused_computation.5 | loop fusion | flops 8 | bytes 48 | tf_op jit(solution)/shard_map/div | solution.py:264
  (5 shorter events, 0.0 us)
Async XLA Ops:
  0.6 11.7 %copy-start.1 = (bf16[4,4096]{1,0:T(4,128)(2,1)S(1)}, bf16[4,4096]{1,0:T(4,128)(2,1)}, u32[]{:S(2)}) copy-start(bf16[4,4096]{1,0:T(4,128)(2,1)} %param.15) | copy-start | bytes 98308
  0.6 6.6 %collective-permute-start = (bf16[4,4096]{1,0:T(4,128)(2,1)}, bf16[4,4096]{1,0:T(4,128)(2,1)S(1)}, u32[]{:S(2)}, u32[]{:S(2)}) collective-permute-start(bf16[4,4096]{1,0:T(4,128)(2,1)} %param.15), channel_id=1, source_target_pairs={{0,8},{1,9},{2,10},{3,11},{4,12},{5,13},{6,14},{7,15},{8,0},{9,1},... | collective-permute-start | bytes 98312 | tf_op jit(solution)/shard_map/ppermute | solution.py:245
  8.0 4.3 %collective-permute-start.1 = (bf16[8,4096]{1,0:T(8,128)(2,1)S(1)}, bf16[8,4096]{1,0:T(8,128)(2,1)S(1)}, u32[]{:S(2)}, u32[]{:S(2)}) collective-permute-start(bf16[8,4096]{1,0:T(8,128)(2,1)S(1)} %pad_maximum_fusion.1), channel_id=1, source_target_pairs={{0,4},{1,5},{2,6},{3,7},{4,0},{5,1},{6,2},{7,3},{8,12},{9,13},{10,... | collective-permute-start | bytes 196616 | tf_op jit(solution)/shard_map/ppermute | solution.py:245
  12.4 5.0 %collective-permute-start.2 = (bf16[16,4096]{1,0:T(8,128)(2,1)S(1)}, bf16[16,4096]{1,0:T(8,128)(2,1)S(1)}, u32[]{:S(2)}, u32[]{:S(2)}) collective-permute-start(bf16[16,4096]{1,0:T(8,128)(2,1)S(1)} %pad_maximum_fusion), channel_id=1, source_target_pairs={{0,2},{1,3},{2,0},{3,1},{4,6},{5,7},{6,4},{7,5},{8,10},{9,11},{10,... | collective-permute-start | bytes 393224 | tf_op jit(solution)/shard_map/ppermute | solution.py:245
  17.4 10.3 %collective-permute-start.3 = (bf16[32,4096]{1,0:T(8,128)(2,1)S(1)}, bf16[32,4096]{1,0:T(8,128)(2,1)S(1)}, u32[]{:S(2)}, u32[]{:S(2)}) collective-permute-start(bf16[32,4096]{1,0:T(8,128)(2,1)S(1)} %constant_dynamic-update-slice_fusion.near_ref), channel_id=1, source_target_pairs={{0,1},{1,0},{2,3},{3,2},{4,5},{5,4},{6,7},{7,6},{8,9},{9,8},{10,11... | collective-permute-start | bytes 786440 | tf_op jit(solution)/shard_map/ppermute | solution.py:245
  27.7 0.8 %copy-start = (bf16[4,4096]{1,0:T(4,128)(2,1)S(1)}, bf16[4,4096]{1,0:T(4,128)(2,1)}, u32[]{:S(2)}) copy-start(bf16[4,4096]{1,0:T(4,128)(2,1)} %shard_map.104.sk_ref) | copy-start | bytes 98308
  29.5 1.3 %collective-permute-start.4 = (f32[32]{0:T(128)S(1)}, f32[32]{0:T(128)S(1)}, u32[]{:S(2)}, u32[]{:S(2)}) collective-permute-start(f32[32]{0:T(128)S(1)} %slice_bitcast_fusion), channel_id=1, source_target_pairs={{0,1},{1,0},{2,3},{3,2},{4,5},{5,4},{6,7},{7,6},{8,9},{9,8},{10,11... | collective-permute-start | bytes 392 | tf_op jit(solution)/shard_map/ppermute | solution.py:245
  30.9 3.5 %collective-permute-start.5 = (f32[16]{0:T(128)S(1)}, f32[16]{0:T(128)S(1)}, u32[]{:S(2)}, u32[]{:S(2)}) collective-permute-start(f32[16]{0:T(128)S(1)} %slice.35), channel_id=1, source_target_pairs={{0,2},{1,3},{2,0},{3,1},{4,6},{5,7},{6,4},{7,5},{8,10},{9,11},{10,... | collective-permute-start | bytes 200 | tf_op jit(solution)/shard_map/ppermute | solution.py:245
  34.6 3.5 %collective-permute-start.6 = (f32[8]{0:T(128)S(1)}, f32[8]{0:T(128)S(1)}, u32[]{:S(2)}, u32[]{:S(2)}) collective-permute-start(f32[8]{0:T(128)S(1)} %slice.37), channel_id=1, source_target_pairs={{0,4},{1,5},{2,6},{3,7},{4,0},{5,1},{6,2},{7,3},{8,12},{9,13},{10,... | collective-permute-start | bytes 104 | tf_op jit(solution)/shard_map/ppermute | solution.py:245
  38.2 4.4 %collective-permute-start.7 = (f32[4]{0:T(128)S(1)}, f32[4]{0:T(128)S(1)}, u32[]{:S(2)}, u32[]{:S(2)}) collective-permute-start(f32[4]{0:T(128)S(1)} %slice.39), channel_id=1, source_target_pairs={{0,8},{1,9},{2,10},{3,11},{4,12},{5,13},{6,14},{7,15},{8,0},{9,1},... | collective-permute-start | bytes 56 | tf_op jit(solution)/shard_map/ppermute | solution.py:245
where the time goes:
time: 43.4 us; the launch traced here: 43.1 us
  waiting for transfers between devices  14.8 us (34%)
  starting transfers between devices  14 us (32%)
  Pallas kernels  11.2 us (26%)
  other arithmetic  1.37 us (3%)
  local copies, waits for them, and re-layouts  1.07 us (2%)
  between operations  0.7 us (2%)
    ppermute x8, waiting for transfers between devices, swap(): return lax.ppermute(v, 'store', [(i, i ^ bit) for i in range(n)])  14.8 us
    ppermute x8, starting transfers between devices, swap(): return lax.ppermute(v, 'store', [(i, i ^ bit) for i in range(n)])  14 us
    pallas_call x1, Pallas kernels, sketch(): pl.pallas_call(functools.partial(kernel, Q=Q, T=T, A=A, W=W), out_shape=j...  10.2 us
    pallas_call x1, Pallas kernels, score(): pl.pallas_call(functools.partial(score_kernel, bits=bits, e=e), out_shape...  0.98 us
  transfers between devices with their start and end apart: 8, of which 7 were waited for; matrix products, arithmetic and copies ran while one was open for 0% of the time, Pallas kernels for 24%

commit v1 on v0

--- a/solution.py
+++ b/solution.py
@@ -9,7 +9,7 @@
 bf = jnp.bfloat16
 f32 = jnp.float32
 NT = (((1,), (1,)), ((), ()))
-VMEM_LIMIT = 60 << 20
+VMEM_LIMIT = 28 << 20
 RADIX = 16
 
 
@@ -114,53 +114,41 @@
     return out
 
 
-def kernel(x_hbm, y_hbm, hi_hbm, si_hbm, ho_hbm, so_hbm, m_hbm, tw_hbm, o_ref,
-           x, h, s, m, tw, bt, cnt, za, zb, p, sem, *, Q, T, A, W):
+def kernel(x, y, hi, si, ho, so, m, tw, o_ref, bt, cx, cy, zx, zy, fr, fi, p, *, Q, T, A, W):
     H, R = A // 2 + 1, Q * T
-    for i, pairs in enumerate((((hi_hbm, h), (si_hbm, s), (x_hbm, x)), ((ho_hbm, h), (so_hbm, s), (y_hbm, x)))):
-        for j, (a, b) in enumerate(pairs):
-            pltpu.make_async_copy(a, b.at[i], sem.at[i, j]).start()
-    tables_in = [pltpu.make_async_copy(tw_hbm, tw, sem.at[2, 0]), pltpu.make_async_copy(m_hbm, m, sem.at[2, 1])]
-    for c in tables_in:
-        c.start()
     p[...] = jnp.zeros_like(p)
 
-    def counts(i, carry):
-        for j, (a, b) in enumerate(((hi_hbm, h), (si_hbm, s), (x_hbm, x))):
-            pltpu.make_async_copy(a, b.at[i], sem.at[i, j]).wait()
-        onehot(h.at[i], bt, W)
-        cnt[i] = count(x.at[i], h.at[i], s.at[i], bt, A, W).reshape(A, R, W)
-        return carry
-
-    lax.fori_loop(0, 2, counts, 0)
-    for c in tables_in:
-        c.wait()
-
-    def rows(q, z):
-        for i in range(2):
-            class_rows(cnt.at[i], q, T, tw, z, i * H * T, A, W)
-
-    def product(q, z):
-        re, im = dft(z[...], m, W)
-        here = lax.broadcasted_iota(jnp.int32, (8, W), 0) == q
-        for k in range(H):
-            a, b = slice(k * T, (k + 1) * T), slice((H + k) * T, (H + k + 1) * T)
-            pr = jnp.sum(re[a] * re[b] - im[a] * im[b], 0, keepdims=True)
-            pi = jnp.sum(re[a] * im[b] + im[a] * re[b], 0, keepdims=True)
-            r = slice(8 * k, 8 * k + 8)
-            p[r, :W] = jnp.where(here, jnp.broadcast_to(pr, (8, W)), p[r, :W])
-            p[r, W:] = jnp.where(here, jnp.broadcast_to(pi, (8, W)), p[r, W:])
-
-    rows(0, za)
-
-    def two(j, carry):
-        rows(2 * j + 1, zb)
-        product(2 * j, za)
-        rows(jnp.minimum(2 * j + 2, Q - 1), za)
-        product(2 * j + 1, zb)
-        return carry
-
-    lax.fori_loop(0, Q // 2, two, 0)
+    def counts(rows_ref, h, s, cnt):
+        onehot(h, bt, W)
+        cnt[...] = count(rows_ref, h, s, bt, A, W).reshape(A, R, W)
+
+    def rows(cnt, z, q0, q1):
+        for q in range(q0, q1):
+            class_rows(cnt, q, T, tw, z, q * H * T, A, W)
+
+    def transform(q0, q1):
+        r = slice(q0 * H * T, q1 * H * T)
+        fr[r, :], fi[r, :] = dft(zx[r, :], m, W)
+
+    def product(q0, q1):
+        re, im = dft(zy[q0 * H * T : q1 * H * T, :], m, W)
+        for q in range(q0, q1):
+            here = lax.broadcasted_iota(jnp.int32, (8, W), 0) == q
+            for k in range(H):
+                a = slice((q * H + k) * T, (q * H + k + 1) * T)
+                b = slice(((q - q0) * H + k) * T, ((q - q0) * H + k + 1) * T)
+                pr = jnp.sum(fr[a, :] * re[b] - fi[a, :] * im[b], 0, keepdims=True)
+                pi = jnp.sum(fr[a, :] * im[b] + fi[a, :] * re[b], 0, keepdims=True)
+                r = slice(8 * k, 8 * k + 8)
+                p[r, :W] = jnp.where(here, jnp.broadcast_to(pr, (8, W)), p[r, :W])
+                p[r, W:] = jnp.where(here, jnp.broadcast_to(pi, (8, W)), p[r, W:])
+
+    counts(x, hi, si, cx)
+    counts(y, ho, so, cy)
+    rows(cx, zx, 0, Q)
+    rows(cy, zy, 0, Q)
+    transform(0, Q)
+    product(0, Q)
     for k, v in enumerate(back(p[...], m, tw, A, W)):
         o_ref[:, k * W : (k + 1) * W] = v[:Q].astype(o_ref.dtype)
 
@@ -182,27 +170,25 @@
 
 def sketch(x, y, hash_in, sign_in, hash_out, sign_out, width):
     Q, T, D = x.shape
-    assert Q <= 8 and Q % 2 == 0 and y.shape[2] == D
     A, W = RADIX, width // RADIX
     H, R = A // 2 + 1, Q * T
+    assert Q <= 8
     m, tw = (jnp.asarray(v) for v in tables(A, W))
     hs = [v.reshape(-1, 128) for v in (hash_in, sign_in, hash_out, sign_out)]
-    x, y = x.reshape(R, D), y.reshape(R, -1)
-    any_ = pl.BlockSpec(memory_space=pl.ANY)
+    vm = pl.BlockSpec(memory_space=pltpu.VMEM)
     return pl.pallas_call(
         functools.partial(kernel, Q=Q, T=T, A=A, W=W),
         out_shape=jax.ShapeDtypeStruct((Q, width), bf),
-        in_specs=[any_] * 8,
-        out_specs=pl.BlockSpec(memory_space=pltpu.VMEM),
+        in_specs=[vm] * 8,
+        out_specs=vm,
         scratch_shapes=[
-            pltpu.VMEM((2, R, D), bf), pltpu.VMEM((2, D // 128, 128), jnp.int32), pltpu.VMEM((2, D // 128, 128), jnp.int32),
-            pltpu.VMEM(m.shape, bf), pltpu.VMEM(tw.shape, f32),
-            pltpu.VMEM((W, D), bf), pltpu.VMEM((2, A, R, W), f32), pltpu.VMEM((2 * H * T, 2 * W), f32), pltpu.VMEM((2 * H * T, 2 * W), f32),
-            pltpu.VMEM((H * 8, 2 * W), f32), pltpu.SemaphoreType.DMA((3, 3)),
+            pltpu.VMEM((W, D), bf), pltpu.VMEM((A, R, W), f32), pltpu.VMEM((A, R, W), f32),
+            pltpu.VMEM((Q * H * T, 2 * W), f32), pltpu.VMEM((Q * H * T, 2 * W), f32),
+            pltpu.VMEM((Q * H * T, W), f32), pltpu.VMEM((Q * H * T, W), f32), pltpu.VMEM((H * 8, 2 * W), f32),
         ],
         cost_estimate=pl.CostEstimate(flops=4 * R * D * width, bytes_accessed=4 << 20, transcendentals=0),
         compiler_params=pltpu.CompilerParams(vmem_limit_bytes=VMEM_LIMIT),
-    )(x, y, *hs, m, tw)
+    )(x.reshape(R, D), y.reshape(R, -1), *hs, m, tw)
 
 
 def score_kernel(me_ref, sk_ref, near_ref, far_ref, s_ref, t_ref, *, bits, e):
@@ -249,14 +235,14 @@
     n = lax.axis_size("store")
     q_dev, e = query_inputs.shape[0], stored.shape[0]
     bits = [1 << b for b in reversed(range(n.bit_length() - 1))]
+    bits = bits[:-2] + [1, 2]
     rows = stored
-    for bit in bits[:-2]:
+    for bit in bits[:-1]:
         rows = jnp.concatenate([rows, swap(rows, bit, n)], 0)
     rows, hash_in = lax.optimization_barrier((rows, hash_in))
-    other = swap(rows, bits[-2], n)
+    far = swap(rows, bits[-1], n)
     sk = sketch(query_inputs, query_grads, hash_in, sign_in, hash_out, sign_out, stored.shape[1])
-    rows = jnp.concatenate([rows, other], 0)
-    scores, t = score(lax.axis_index("store"), sk, rows, swap(rows, bits[-1], n), bits)
+    scores, t = score(lax.axis_index("store"), sk, rows, far, bits)
     t = t.reshape(-1)
     for bit in reversed(bits):
         half = t.shape[0] // 2

time: 43.4 us -> 40.1 us (0.924)
  Pallas kernels: 11.2 us -> 8.34 us
  starting transfers between devices: 14 us -> 11.7 us
  local copies, waits for them, and re-layouts: 1.07 us -> 2.6 us
    pallas_call x1, Pallas kernels: 10.2 us -> 7.35 us  [sketch(): pl.pallas_call(functools.partial(kernel, Q=Q, T=T, A=A, W=W), out_shape=j...]
    ppermute x8, starting transfers between devices: 14 us -> 11.7 us  [swap(): return lax.ppermute(v, 'store', [(i, i ^ bit) for i in range(n)])]
    unnamed x5 -> x18, local copies, waits for them, and re-layouts: 0.76 us -> 2.3 us
    concatenate x2 -> x3, other arithmetic: 0.85 us -> 0.91 us  [body(): rows = jnp.concatenate([rows, swap(rows, bit, n)], 0)]
  transfers between devices with their start and end apart: 8 -> 8, of which waited for: 7 -> 7; matrix products, arithmetic and copies ran while one was open for 0% -> 0% of each run, Pallas kernels for 24% -> 18%
where the time goes in v1:
time: 40.1 us; the launch traced here: 39.8 us
  waiting for transfers between devices  15 us (37%)
  starting transfers between devices  11.7 us (29%)
  Pallas kernels  8.34 us (21%)
  local copies, waits for them, and re-layouts  2.6 us (6%)
  other arithmetic  1.43 us (4%)
  between operations  0.77 us (2%)
    ppermute x8, waiting for transfers between devices, swap(): return lax.ppermute(v, 'store', [(i, i ^ bit) for i in range(n)])  15 us
    ppermute x8, starting transfers between devices, swap(): return lax.ppermute(v, 'store', [(i, i ^ bit) for i in range(n)])  11.7 us
    pallas_call x1, Pallas kernels, sketch(): pl.pallas_call(functools.partial(kernel, Q=Q, T=T, A=A, W=W), out_shape=j...  7.35 us
    unnamed x18, local copies, waits for them, and re-layouts  2.3 us
    pallas_call x1, Pallas kernels, score(): pl.pallas_call(functools.partial(score_kernel, bits=bits, e=e), out_shape...  0.99 us
    concatenate x3, other arithmetic, body(): rows = jnp.concatenate([rows, swap(rows, bit, n)], 0)  0.91 us
  transfers between devices with their start and end apart: 8, of which 7 were waited for; matrix products, arithmetic and copies ran while one was open for 0% of the time, Pallas kernels for 18%

profile of v1, /device:TPU:0, one launch (start us, length us, event | category | flops | bytes accessed | tf_op | source)
XLA Modules:
  0.0 39.8 jit_solution(10492922818557770741)
XLA Ops:
  0.6 0.0 copy-start.8
  0.6 0.0 copy-start
  0.6 4.1 %collective-permute-start = (bf16[4,4096]{1,0:T(4,128)(2,1)}, bf16[4,4096]{1,0:T(4,128)(2,1)S(1)}, u32[]{:S(2)}, u32[]{:S(2)}) collective-permute-start(bf16[4,4096]{1,0:T(4,128)(2,1)} %param.15), channel_id=1, source_target_pairs={{0,8},{1,9},{2,10},{3,11},{4,12},{5,13},{6,14},{7,15},{8,0},{9,1},... | collective-permute-start | bytes 98312 | tf_op jit(solution)/shard_map/ppermute | solution.py:231
  4.8 2.5 %collective-permute-done = bf16[4,4096]{1,0:T(4,128)(2,1)S(1)} collective-permute-done((bf16[4,4096]{1,0:T(4,128)(2,1)}, bf16[4,4096]{1,0:T(4,128)(2,1)S(1)}, u32[]{:S(2)}, u32[]{:S(2)}) %collective-permute-start) | collective-permute-done | bytes 32800 | tf_op jit(solution)/shard_map/ppermute | solution.py:231
  7.2 0.8 %pad_maximum_fusion.2 = bf16[8,4096]{1,0:T(8,128)(2,1)S(1)} fusion(bf16[4,4096]{1,0:T(4,128)(2,1)S(1)} %collective-permute-done, bf16[4,4096]{1,0:T(4,128)(2,1)} %param.15), kind=kLoop, calls=%fused_computation.2 | loop fusion | flops 131072 | bytes 131072 | tf_op jit(solution)/shard_map/concatenate | solution.py:241
  8.0 1.6 %collective-permute-start.1 = (bf16[8,4096]{1,0:T(8,128)(2,1)S(1)}, bf16[8,4096]{1,0:T(8,128)(2,1)S(1)}, u32[]{:S(2)}, u32[]{:S(2)}) collective-permute-start(bf16[8,4096]{1,0:T(8,128)(2,1)S(1)} %pad_maximum_fusion.2), channel_id=1, source_target_pairs={{0,4},{1,5},{2,6},{3,7},{4,0},{5,1},{6,2},{7,3},{8,12},{9,13},{10,... | collective-permute-start | bytes 196616 | tf_op jit(solution)/shard_map/ppermute | solution.py:231
  9.6 2.7 %collective-permute-done.1 = bf16[8,4096]{1,0:T(8,128)(2,1)S(1)} collective-permute-done((bf16[8,4096]{1,0:T(8,128)(2,1)S(1)}, bf16[8,4096]{1,0:T(8,128)(2,1)S(1)}, u32[]{:S(2)}, u32[]{:S(2)}) %collective-permute-start.1) | collective-permute-done | bytes 65568 | tf_op jit(solution)/shard_map/ppermute | solution.py:231
  12.3 0.0 copy-done.8
  12.3 0.1 pad_maximum_fusion.1
  12.4 0.1 collective-permute-start.2
  12.5 0.0 copy-start.2
  12.5 0.0 copy-start.3
  12.5 0.0 copy-start.4
  12.5 0.0 copy-start.5
  12.5 0.0 copy-start.7
  12.5 1.3 %collective-permute-done.2 = bf16[16,4096]{1,0:T(8,128)(2,1)S(1)} collective-permute-done((bf16[16,4096]{1,0:T(8,128)(2,1)S(1)}, bf16[16,4096]{1,0:T(8,128)(2,1)S(1)}, u32[]{:S(2)}, u32[]{:S(2)}) %collective-permute-start.2) | collective-permute-done | bytes 131104 | tf_op jit(solution)/shard_map/ppermute | solution.py:231
  13.8 0.1 pad_maximum_fusion.near_ref
  13.9 1.8 %collective-permute-start.3 = (bf16[32,4096]{1,0:T(8,128)(2,1)S(1)}, bf16[32,4096]{1,0:T(8,128)(2,1)S(1)}, u32[]{:S(2)}, u32[]{:S(2)}) collective-permute-start(bf16[32,4096]{1,0:T(8,128)(2,1)S(1)} %pad_maximum_fusion.near_ref), channel_id=1, source_target_pairs={{0,2},{1,3},{2,0},{3,1},{4,6},{5,7},{6,4},{7,5},{8,10},{9,11},{10,... | collective-permute-start | bytes 786440 | tf_op jit(solution)/shard_map/ppermute | solution.py:231
  15.7 0.0 copy-done
  15.7 0.0 copy-done.2
  15.7 0.0 copy-done.3
  15.7 0.0 copy-done.4
  15.7 0.0 copy-done.5
  15.7 0.0 copy-done.7
  15.7 0.0 copy-start.1
  15.7 1.0 %copy-done.1 = bf16[4,16,4096]{2,1,0:T(8,128)(2,1)S(1)} copy-done((bf16[4,16,4096]{2,1,0:T(8,128)(2,1)S(1)}, bf16[4,16,4096]{2,1,0:T(8,128)(2,1)}, u32[]{:S(2)}) %copy-start.1) | copy-done | bytes 524312
  16.7 0.0 copy-start.6
  16.7 1.2 %copy-done.6 = bf16[1024,512]{1,0:T(8,128)(2,1)S(1)} copy-done((bf16[1024,512]{1,0:T(8,128)(2,1)S(1)}, bf16[1024,512]{1,0:T(8,128)(2,1)}, u32[]{:S(2)}) %copy-start.6) | copy-done | bytes 1048600
  18.0 7.4 %shard_map.104.sk_ref = bf16[4,4096]{1,0:T(4,128)(2,1)S(1)} custom-call(bf16[64,4096]{1,0:T(8,128)(2,1)S(1)} %bitcast.11, bf16[64,4096]{1,0:T(8,128)(2,1)S(1)} %bitcast.12, s32[32,128]{1,0:T(8,128)S(1)} %bitcast.13, s32[32,128]{1,0:T(8,128)S(1)} %bitcast.14, s32[32,128]{1,0:T(8,128)S(1)} %bitcast.15, s32[32,128]{1,0:T(8,128)S(1)} %bitcast.16, ...), custom_call_target="tpu_custom_call" | custom-call | flops 4294967296 | bytes 4194304 | tf_op jit(solution)/shard_map/pallas_call | solution.py:179
  25.3 0.0 collective-permute-done.3.far_ref
  25.3 1.0 %shard_map.105 = (f32[4,64]{1,0:T(4,128)}, f32[1,64]{1,0:T(1,128)S(1)}) custom-call(s32[1]{0:T(128)} %bitcast.me_ref, bf16[4,4096]{1,0:T(4,128)(2,1)S(1)} %shard_map.104.sk_ref, bf16[32,4096]{1,0:T(8,128)(2,1)S(1)} %pad_maximum_fusion.near_ref, bf16[32,4096]{1,0:T(8,128)(2,1)S(1)} %collective-permute-done.3.far_ref), custom_call_target="tpu_custom_call" | custom-call | flops 2097152 | bytes 524288 | tf_op jit(solution)/shard_map/pallas_call | solution.py:220
  26.3 0.1 slice_bitcast_fusion
  26.4 0.3 collective-permute-start.4
  26.7 3.2 %collective-permute-done.4 = f32[32]{0:T(128)S(1)} collective-permute-done((f32[32]{0:T(128)S(1)}, f32[32]{0:T(128)S(1)}, u32[]{:S(2)}, u32[]{:S(2)}) %collective-permute-start.4) | collective-permute-done | bytes 160 | tf_op jit(solution)/shard_map/ppermute | solution.py:231
  29.9 0.1 slice.35
  30.0 0.0 collective-permute-start.5
  30.0 1.1 %collective-permute-done.5 = f32[16]{0:T(128)S(1)} collective-permute-done((f32[16]{0:T(128)S(1)}, f32[16]{0:T(128)S(1)}, u32[]{:S(2)}, u32[]{:S(2)}) %collective-permute-start.5) | collective-permute-done | bytes 96 | tf_op jit(solution)/shard_map/ppermute | solution.py:231
  31.1 0.1 slice.37
  31.2 1.4 %collective-permute-start.6 = (f32[8]{0:T(128)S(1)}, f32[8]{0:T(128)S(1)}, u32[]{:S(2)}, u32[]{:S(2)}) collective-permute-start(f32[8]{0:T(128)S(1)} %slice.37), channel_id=1, source_target_pairs={{0,4},{1,5},{2,6},{3,7},{4,0},{5,1},{6,2},{7,3},{8,12},{9,13},{10,... | collective-permute-start | bytes 104 | tf_op jit(solution)/shard_map/ppermute | solution.py:231
  32.6 2.2 %collective-permute-done.6 = f32[8]{0:T(128)S(1)} collective-permute-done((f32[8]{0:T(128)S(1)}, f32[8]{0:T(128)S(1)}, u32[]{:S(2)}, u32[]{:S(2)}) %collective-permute-start.6) | collective-permute-done | bytes 64 | tf_op jit(solution)/shard_map/ppermute | solution.py:231
  34.8 0.1 slice.39
  34.8 2.4 %collective-permute-start.7 = (f32[4]{0:T(128)S(1)}, f32[4]{0:T(128)S(1)}, u32[]{:S(2)}, u32[]{:S(2)}) collective-permute-start(f32[4]{0:T(128)S(1)} %slice.39), channel_id=1, source_target_pairs={{0,8},{1,9},{2,10},{3,11},{4,12},{5,13},{6,14},{7,15},{8,0},{9,1},... | collective-permute-start | bytes 56 | tf_op jit(solution)/shard_map/ppermute | solution.py:231
  37.2 2.0 %collective-permute-done.7 = f32[4]{0:T(128)S(1)} collective-permute-done((f32[4]{0:T(128)S(1)}, f32[4]{0:T(128)S(1)}, u32[]{:S(2)}, u32[]{:S(2)}) %collective-permute-start.7) | collective-permute-done | bytes 48 | tf_op jit(solution)/shard_map/ppermute | solution.py:231
  39.3 0.5 %add_multiply_fusion = f32[4]{0:T(128)} fusion(f32[4]{0:T(128)S(1)} %collective-permute-done.7, f32[8]{0:T(128)S(1)} %slice_add_fusion), kind=kLoop, calls=%fused_computation.4 | loop fusion | flops 8 | bytes 48 | tf_op jit(solution)/shard_map/div | solution.py:250
  (3 shorter events, 0.0 us)
Async XLA Ops:
  0.6 11.7 %copy-start.8 = (bf16[4,4096]{1,0:T(4,128)(2,1)S(1)}, bf16[4,4096]{1,0:T(4,128)(2,1)}, u32[]{:S(2)}) copy-start(bf16[4,4096]{1,0:T(4,128)(2,1)} %param.15) | copy-start | bytes 98308
  0.6 15.0 %copy-start = (bf16[4,16,4096]{2,1,0:T(8,128)(2,1)S(1)}, bf16[4,16,4096]{2,1,0:T(8,128)(2,1)}, u32[]{:S(2)}) copy-start(bf16[4,16,4096]{2,1,0:T(8,128)(2,1)} %param.9) | copy-start | bytes 1572868
  0.6 6.6 %collective-permute-start = (bf16[4,4096]{1,0:T(4,128)(2,1)}, bf16[4,4096]{1,0:T(4,128)(2,1)S(1)}, u32[]{:S(2)}, u32[]{:S(2)}) collective-permute-start(bf16[4,4096]{1,0:T(4,128)(2,1)} %param.15), channel_id=1, source_target_pairs={{0,8},{1,9},{2,10},{3,11},{4,12},{5,13},{6,14},{7,15},{8,0},{9,1},... | collective-permute-start | bytes 98312 | tf_op jit(solution)/shard_map/ppermute | solution.py:231
  8.0 4.3 %collective-permute-start.1 = (bf16[8,4096]{1,0:T(8,128)(2,1)S(1)}, bf16[8,4096]{1,0:T(8,128)(2,1)S(1)}, u32[]{:S(2)}, u32[]{:S(2)}) collective-permute-start(bf16[8,4096]{1,0:T(8,128)(2,1)S(1)} %pad_maximum_fusion.2), channel_id=1, source_target_pairs={{0,4},{1,5},{2,6},{3,7},{4,0},{5,1},{6,2},{7,3},{8,12},{9,13},{10,... | collective-permute-start | bytes 196616 | tf_op jit(solution)/shard_map/ppermute | solution.py:231
  12.4 1.4 %collective-permute-start.2 = (bf16[16,4096]{1,0:T(8,128)(2,1)S(1)}, bf16[16,4096]{1,0:T(8,128)(2,1)S(1)}, u32[]{:S(2)}, u32[]{:S(2)}) collective-permute-start(bf16[16,4096]{1,0:T(8,128)(2,1)S(1)} %pad_maximum_fusion.1), channel_id=1, source_target_pairs={{0,1},{1,0},{2,3},{3,2},{4,5},{5,4},{6,7},{7,6},{8,9},{9,8},{10,11... | collective-permute-start | bytes 393224 | tf_op jit(solution)/shard_map/ppermute | solution.py:231
  12.5 3.2 %copy-start.2 = (s32[4096]{0:T(1024)S(1)}, s32[4096]{0:T(1024)}, u32[]{:S(2)}) copy-start(s32[4096]{0:T(1024)} %param.11) | copy-start | bytes 49156
  12.5 3.2 %copy-start.3 = (s32[4096]{0:T(1024)S(1)}, s32[4096]{0:T(1024)}, u32[]{:S(2)}) copy-start(s32[4096]{0:T(1024)} %param.12) | copy-start | bytes 49156
  12.5 3.2 %copy-start.4 = (s32[4096]{0:T(1024)S(1)}, s32[4096]{0:T(1024)}, u32[]{:S(2)}) copy-start(s32[4096]{0:T(1024)} %param.13) | copy-start | bytes 49156
  12.5 3.2 %copy-start.5 = (s32[4096]{0:T(1024)S(1)}, s32[4096]{0:T(1024)}, u32[]{:S(2)}) copy-start(s32[4096]{0:T(1024)} %param.14) | copy-start | bytes 49156
  12.5 3.2 %copy-start.7 = (f32[24,256]{1,0:T(8,128)S(1)}, f32[24,256]{1,0:T(8,128)}, u32[]{:S(2)}) copy-start(f32[24,256]{1,0:T(8,128)} %constant.12.clone.tw) | copy-start | bytes 73732
  13.9 11.5 %collective-permute-start.3 = (bf16[32,4096]{1,0:T(8,128)(2,1)S(1)}, bf16[32,4096]{1,0:T(8,128)(2,1)S(1)}, u32[]{:S(2)}, u32[]{:S(2)}) collective-permute-start(bf16[32,4096]{1,0:T(8,128)(2,1)S(1)} %pad_maximum_fusion.near_ref), channel_id=1, source_target_pairs={{0,2},{1,3},{2,0},{3,1},{4,6},{5,7},{6,4},{7,5},{8,10},{9,11},{10,... | collective-permute-start | bytes 786440 | tf_op jit(solution)/shard_map/ppermute | solution.py:231
  15.7 1.0 %copy-start.1 = (bf16[4,16,4096]{2,1,0:T(8,128)(2,1)S(1)}, bf16[4,16,4096]{2,1,0:T(8,128)(2,1)}, u32[]{:S(2)}) copy-start(bf16[4,16,4096]{2,1,0:T(8,128)(2,1)} %param.10) | copy-start | bytes 1572868
  16.7 1.2 %copy-start.6 = (bf16[1024,512]{1,0:T(8,128)(2,1)S(1)}, bf16[1024,512]{1,0:T(8,128)(2,1)}, u32[]{:S(2)}) copy-start(bf16[1024,512]{1,0:T(8,128)(2,1)} %constant.11.clone.m) | copy-start | bytes 3145732
  26.4 3.5 %collective-permute-start.4 = (f32[32]{0:T(128)S(1)}, f32[32]{0:T(128)S(1)}, u32[]{:S(2)}, u32[]{:S(2)}) collective-permute-start(f32[32]{0:T(128)S(1)} %slice_bitcast_fusion), channel_id=1, source_target_pairs={{0,2},{1,3},{2,0},{3,1},{4,6},{5,7},{6,4},{7,5},{8,10},{9,11},{10,... | collective-permute-start | bytes 392 | tf_op jit(solution)/shard_map/ppermute | solution.py:231
  30.0 1.1 %collective-permute-start.5 = (f32[16]{0:T(128)S(1)}, f32[16]{0:T(128)S(1)}, u32[]{:S(2)}, u32[]{:S(2)}) collective-permute-start(f32[16]{0:T(128)S(1)} %slice.35), channel_id=1, source_target_pairs={{0,1},{1,0},{2,3},{3,2},{4,5},{5,4},{6,7},{7,6},{8,9},{9,8},{10,11... | collective-permute-start | bytes 200 | tf_op jit(solution)/shard_map/ppermute | solution.py:231
  31.2 3.5 %collective-permute-start.6 = (f32[8]{0:T(128)S(1)}, f32[8]{0:T(128)S(1)}, u32[]{:S(2)}, u32[]{:S(2)}) collective-permute-start(f32[8]{0:T(128)S(1)} %slice.37), channel_id=1, source_target_pairs={{0,4},{1,5},{2,6},{3,7},{4,0},{5,1},{6,2},{7,3},{8,12},{9,13},{10,... | collective-permute-start | bytes 104 | tf_op jit(solution)/shard_map/ppermute | solution.py:231
  34.8 4.4 %collective-permute-start.7 = (f32[4]{0:T(128)S(1)}, f32[4]{0:T(128)S(1)}, u32[]{:S(2)}, u32[]{:S(2)}) collective-permute-start(f32[4]{0:T(128)S(1)} %slice.39), channel_id=1, source_target_pairs={{0,8},{1,9},{2,10},{3,11},{4,12},{5,13},{6,14},{7,15},{8,0},{9,1},... | collective-permute-start | bytes 56 | tf_op jit(solution)/shard_map/ppermute | solution.py:231

commit v2 on v1

--- a/solution.py
+++ b/solution.py
@@ -9,7 +9,7 @@
 bf = jnp.bfloat16
 f32 = jnp.float32
 NT = (((1,), (1,)), ((), ()))
-VMEM_LIMIT = 28 << 20
+VMEM_LIMIT = 24 << 20
 RADIX = 16
 
 
@@ -114,41 +114,35 @@
     return out
 
 
-def kernel(x, y, hi, si, ho, so, m, tw, o_ref, bt, cx, cy, zx, zy, fr, fi, p, *, Q, T, A, W):
-    H, R = A // 2 + 1, Q * T
+def count_kernel(*refs, Q, T, A, W):
+    given, (cx, cy, x, y, hi, si, ho, so, bt, sem) = refs[:6], refs[6:]
+    copies = [pltpu.make_async_copy(a, b, sem.at[i]) for i, (a, b) in enumerate(zip(given, (hi, si, x, ho, so, y)))]
+    for c in copies:
+        c.start()
+    for c in copies:
+        c.wait()
+    for rows_ref, h, s, cnt in ((x, hi, si, cx), (y, ho, so, cy)):
+        onehot(h, bt, W)
+        cnt[...] = count(rows_ref, h, s, bt, A, W).reshape(A, Q * T, W)
+
+
+def sketch_kernel(cx, cy, m, tw, o_ref, zx, zy, fr, fi, p, *, Q, T, A, W):
+    H = A // 2 + 1
     p[...] = jnp.zeros_like(p)
-
-    def counts(rows_ref, h, s, cnt):
-        onehot(h, bt, W)
-        cnt[...] = count(rows_ref, h, s, bt, A, W).reshape(A, R, W)
-
-    def rows(cnt, z, q0, q1):
-        for q in range(q0, q1):
+    for cnt, z in ((cx, zx), (cy, zy)):
+        for q in range(Q):
             class_rows(cnt, q, T, tw, z, q * H * T, A, W)
-
-    def transform(q0, q1):
-        r = slice(q0 * H * T, q1 * H * T)
-        fr[r, :], fi[r, :] = dft(zx[r, :], m, W)
-
-    def product(q0, q1):
-        re, im = dft(zy[q0 * H * T : q1 * H * T, :], m, W)
-        for q in range(q0, q1):
-            here = lax.broadcasted_iota(jnp.int32, (8, W), 0) == q
-            for k in range(H):
-                a = slice((q * H + k) * T, (q * H + k + 1) * T)
-                b = slice(((q - q0) * H + k) * T, ((q - q0) * H + k + 1) * T)
-                pr = jnp.sum(fr[a, :] * re[b] - fi[a, :] * im[b], 0, keepdims=True)
-                pi = jnp.sum(fr[a, :] * im[b] + fi[a, :] * re[b], 0, keepdims=True)
-                r = slice(8 * k, 8 * k + 8)
-                p[r, :W] = jnp.where(here, jnp.broadcast_to(pr, (8, W)), p[r, :W])
-                p[r, W:] = jnp.where(here, jnp.broadcast_to(pi, (8, W)), p[r, W:])
-
-    counts(x, hi, si, cx)
-    counts(y, ho, so, cy)
-    rows(cx, zx, 0, Q)
-    rows(cy, zy, 0, Q)
-    transform(0, Q)
-    product(0, Q)
+    fr[...], fi[...] = dft(zx[...], m, W)
+    re, im = dft(zy[...], m, W)
+    for q in range(Q):
+        here = lax.broadcasted_iota(jnp.int32, (8, W), 0) == q
+        for k in range(H):
+            a = slice((q * H + k) * T, (q * H + k + 1) * T)
+            pr = jnp.sum(fr[a, :] * re[a] - fi[a, :] * im[a], 0, keepdims=True)
+            pi = jnp.sum(fr[a, :] * im[a] + fi[a, :] * re[a], 0, keepdims=True)
+            r = slice(8 * k, 8 * k + 8)
+            p[r, :W] = jnp.where(here, jnp.broadcast_to(pr, (8, W)), p[r, :W])
+            p[r, W:] = jnp.where(here, jnp.broadcast_to(pi, (8, W)), p[r, W:])
     for k, v in enumerate(back(p[...], m, tw, A, W)):
         o_ref[:, k * W : (k + 1) * W] = v[:Q].astype(o_ref.dtype)
 
@@ -168,27 +162,41 @@
     return irfft(X)
 
 
-def sketch(x, y, hash_in, sign_in, hash_out, sign_out, width):
+def counts(x, y, hash_in, sign_in, hash_out, sign_out, width):
     Q, T, D = x.shape
     A, W = RADIX, width // RADIX
-    H, R = A // 2 + 1, Q * T
+    hi, si, ho, so = (v.reshape(-1, 128) for v in (hash_in, sign_in, hash_out, sign_out))
+    x, y = x.reshape(Q * T, D), y.reshape(Q * T, -1)
+    vm = pl.BlockSpec(memory_space=pltpu.VMEM)
+    return pl.pallas_call(
+        functools.partial(count_kernel, Q=Q, T=T, A=A, W=W),
+        out_shape=(jax.ShapeDtypeStruct((A, Q * T, W), f32),) * 2,
+        in_specs=[pl.BlockSpec(memory_space=pltpu.HBM)] * 6,
+        out_specs=(vm, vm),
+        scratch_shapes=[pltpu.VMEM(v.shape, v.dtype) for v in (x, y, hi, si, ho, so)] + [pltpu.VMEM((W, D), bf), pltpu.SemaphoreType.DMA((6,))],
+        cost_estimate=pl.CostEstimate(flops=4 * Q * T * D * width, bytes_accessed=4 << 20, transcendentals=0),
+        compiler_params=pltpu.CompilerParams(vmem_limit_bytes=VMEM_LIMIT),
+    )(*(pltpu.with_memory_space_constraint(v, pltpu.HBM) for v in (hi, si, x, ho, so, y)))
+
+
+def sketch(cx, cy, Q):
+    A, R, W = cx.shape
+    T, H = R // Q, A // 2 + 1
     assert Q <= 8
     m, tw = (jnp.asarray(v) for v in tables(A, W))
-    hs = [v.reshape(-1, 128) for v in (hash_in, sign_in, hash_out, sign_out)]
     vm = pl.BlockSpec(memory_space=pltpu.VMEM)
     return pl.pallas_call(
-        functools.partial(kernel, Q=Q, T=T, A=A, W=W),
-        out_shape=jax.ShapeDtypeStruct((Q, width), bf),
-        in_specs=[vm] * 8,
+        functools.partial(sketch_kernel, Q=Q, T=T, A=A, W=W),
+        out_shape=jax.ShapeDtypeStruct((Q, A * W), bf),
+        in_specs=[vm] * 4,
         out_specs=vm,
         scratch_shapes=[
-            pltpu.VMEM((W, D), bf), pltpu.VMEM((A, R, W), f32), pltpu.VMEM((A, R, W), f32),
             pltpu.VMEM((Q * H * T, 2 * W), f32), pltpu.VMEM((Q * H * T, 2 * W), f32),
             pltpu.VMEM((Q * H * T, W), f32), pltpu.VMEM((Q * H * T, W), f32), pltpu.VMEM((H * 8, 2 * W), f32),
         ],
-        cost_estimate=pl.CostEstimate(flops=4 * R * D * width, bytes_accessed=4 << 20, transcendentals=0),
+        cost_estimate=pl.CostEstimate(flops=1 << 32, bytes_accessed=4 << 20, transcendentals=0),
         compiler_params=pltpu.CompilerParams(vmem_limit_bytes=VMEM_LIMIT),
-    )(x.reshape(R, D), y.reshape(R, -1), *hs, m, tw)
+    )(cx, cy, m, tw)
 
 
 def score_kernel(me_ref, sk_ref, near_ref, far_ref, s_ref, t_ref, *, bits, e):
@@ -235,14 +243,16 @@
     n = lax.axis_size("store")
     q_dev, e = query_inputs.shape[0], stored.shape[0]
     bits = [1 << b for b in reversed(range(n.bit_length() - 1))]
-    bits = bits[:-2] + [1, 2]
-    rows = stored
-    for bit in bits[:-1]:
+    first, second = bits[:2]
+    parts = [stored] + [swap(stored, bit, n) for bit in (first, second, first ^ second)]
+    cx, cy = counts(query_inputs, query_grads, hash_in, sign_in, hash_out, sign_out, stored.shape[1])
+    rows, cx = lax.optimization_barrier((jnp.concatenate(parts, 0), cx))
+    for bit in bits[2:-2]:
         rows = jnp.concatenate([rows, swap(rows, bit, n)], 0)
-    rows, hash_in = lax.optimization_barrier((rows, hash_in))
-    far = swap(rows, bits[-1], n)
-    sk = sketch(query_inputs, query_grads, hash_in, sign_in, hash_out, sign_out, stored.shape[1])
-    scores, t = score(lax.axis_index("store"), sk, rows, far, bits)
+    other = swap(rows, bits[-2], n)
+    sk = sketch(cx, cy, q_dev)
+    rows, sk = lax.optimization_barrier((jnp.concatenate([rows, other], 0), sk))
+    scores, t = score(lax.axis_index("store"), sk, rows, swap(rows, bits[-1], n), bits)
     t = t.reshape(-1)
     for bit in reversed(bits):
         half = t.shape[0] // 2

time: 40.1 us -> 34.2 us (0.85)
  waiting for transfers between devices: 15 us -> 9.51 us
  local copies, waits for them, and re-layouts: 2.6 us -> 0.31 us
  Pallas kernels: 8.34 us -> 10.2 us
  starting transfers between devices: 11.7 us -> 12.7 us
  other arithmetic: 1.43 us -> 0.63 us
    ppermute x8 -> x9, waiting for transfers between devices: 15 us -> 9.51 us  [swap(): return lax.ppermute(v, 'store', [(i, i ^ bit) for i in range(n)])]
    unnamed x18 -> x6, local copies, waits for them, and re-layouts: 2.3 us -> 0.01 us
    pallas_call x1 -> x2, Pallas kernels: 7.35 us -> 9.23 us  [the longest x1 6.49 us: counts(): pl.pallas_call(functools.partial(count_kernel, Q=Q, T=T, A=A, W=W), out_s...]
    ppermute x8 -> x9, starting transfers between devices: 11.7 us -> 12.7 us  [swap(): return lax.ppermute(v, 'store', [(i, i ^ bit) for i in range(n)])]
    concatenate x3 -> x2, other arithmetic: 0.91 us -> 0.1 us  [the longest x1 0.08 us: body(): rows, cx = lax.optimization_barrier((jnp.concatenate(parts, 0), cx))]
  transfers between devices with their start and end apart: 8 -> 9, of which waited for: 7 -> 6; matrix products, arithmetic and copies ran while one was open for 0% -> 0% of each run, Pallas kernels for 18% -> 27%
where the time goes in v2:
time: 34.2 us; the launch traced here: 34.1 us
  starting transfers between devices  12.7 us (37%)
  Pallas kernels  10.2 us (30%)
  waiting for transfers between devices  9.51 us (28%)
  between operations  0.72 us (2%)
  other arithmetic  0.63 us (2%)
    ppermute x9, starting transfers between devices, swap(): return lax.ppermute(v, 'store', [(i, i ^ bit) for i in range(n)])  12.7 us
    ppermute x9, waiting for transfers between devices, swap(): return lax.ppermute(v, 'store', [(i, i ^ bit) for i in range(n)])  9.51 us
    pallas_call x1, Pallas kernels, counts(): pl.pallas_call(functools.partial(count_kernel, Q=Q, T=T, A=A, W=W), out_s...  6.49 us
    pallas_call x1, Pallas kernels, sketch(): pl.pallas_call(functools.partial(sketch_kernel, Q=Q, T=T, A=A, W=W), out_...  2.74 us
    pallas_call x1, Pallas kernels, score(): pl.pallas_call(functools.partial(score_kernel, bits=bits, e=e), out_shape...  0.98 us
  transfers between devices with their start and end apart: 9, of which 6 were waited for; matrix products, arithmetic and copies ran while one was open for 0% of the time, Pallas kernels for 27%

profile of v2, /device:TPU:0, one launch (start us, length us, event | category | flops | bytes accessed | tf_op | source)
XLA Modules:
  0.0 34.1 jit_solution(4826520892544636613)
XLA Ops:
  0.6 3.1 %collective-permute-start.1 = (bf16[4,4096]{1,0:T(4,128)(2,1)}, bf16[4,4096]{1,0:T(4,128)(2,1)S(1)}, u32[]{:S(2)}, u32[]{:S(2)}) collective-permute-start(bf16[4,4096]{1,0:T(4,128)(2,1)} %param.15), channel_id=1, source_target_pairs={{0,4},{1,5},{2,6},{3,7},{4,0},{5,1},{6,2},{7,3},{8,12},{9,13},{10,... | collective-permute-start | bytes 98312 | tf_op jit(solution)/shard_map/ppermute | solution.py:239
  3.7 2.6 %collective-permute-start = (bf16[4,4096]{1,0:T(4,128)(2,1)}, bf16[4,4096]{1,0:T(4,128)(2,1)S(1)}, u32[]{:S(2)}, u32[]{:S(2)}) collective-permute-start(bf16[4,4096]{1,0:T(4,128)(2,1)} %param.15), channel_id=1, source_target_pairs={{0,8},{1,9},{2,10},{3,11},{4,12},{5,13},{6,14},{7,15},{8,0},{9,1},... | collective-permute-start | bytes 98312 | tf_op jit(solution)/shard_map/ppermute | solution.py:239
  6.3 0.0 collective-permute-start.2
  6.3 0.0 copy-start.2
  6.3 0.0 copy-start
  6.3 6.5 %shard_map.104 = (f32[16,64,256]{2,1,0:T(8,128)S(1)}, f32[16,64,256]{2,1,0:T(8,128)S(1)}) custom-call(s32[32,128]{1,0:T(8,128)} %bitcast.13, s32[32,128]{1,0:T(8,128)} %bitcast.14, bf16[64,4096]{1,0:T(8,128)(2,1)} %bitcast.11, s32[32,128]{1,0:T(8,128)} %bitcast.15, s32[32,128]{1,0:T(8,128)} %bitcast.16, bf16[64,4096]{1,0:T(8,128)(2,1)} %bitcast.12), custom_call_target="tpu_custom_call" | custom-call | flops 4294967296 | bytes 4194304 | tf_op jit(solution)/shard_map/pallas_call | solution.py:171
  12.8 0.0 copy-start.1
  12.8 0.0 collective-permute-done.1
  12.8 0.0 collective-permute-done
  12.8 0.0 collective-permute-done.2
  12.9 0.0 copy-done.2
  12.9 0.1 pad_maximum_fusion.1
  13.0 1.8 %collective-permute-start.3 = (bf16[16,4096]{1,0:T(8,128)(2,1)S(1)}, bf16[16,4096]{1,0:T(8,128)(2,1)S(1)}, u32[]{:S(2)}, u32[]{:S(2)}) collective-permute-start(bf16[16,4096]{1,0:T(8,128)(2,1)S(1)} %pad_maximum_fusion.1), channel_id=1, source_target_pairs={{0,2},{1,3},{2,0},{3,1},{4,6},{5,7},{6,4},{7,5},{8,10},{9,11},{10,... | collective-permute-start | bytes 393224 | tf_op jit(solution)/shard_map/ppermute | solution.py:239
  14.8 0.0 copy-done
  14.8 0.0 copy-done.1
  14.8 2.7 %shard_map.105.sk_ref = bf16[4,4096]{1,0:T(4,128)(2,1)S(1)} custom-call(f32[16,64,256]{2,1,0:T(8,128)S(1)} %get-tuple-element.12.cx, f32[16,64,256]{2,1,0:T(8,128)S(1)} %get-tuple-element.13.cy, bf16[1024,512]{1,0:T(8,128)(2,1)S(1)} %copy-done, f32[24,256]{1,0:T(8,128)S(1)} %copy-done.1), custom_call_target="tpu_custom_call" | custom-call | flops 4294967296 | bytes 4194304 | tf_op jit(solution)/shard_map/pallas_call | solution.py:188
  17.5 0.5 %collective-permute-done.3 = bf16[16,4096]{1,0:T(8,128)(2,1)S(1)} collective-permute-done((bf16[16,4096]{1,0:T(8,128)(2,1)S(1)}, bf16[16,4096]{1,0:T(8,128)(2,1)S(1)}, u32[]{:S(2)}, u32[]{:S(2)}) %collective-permute-start.3) | collective-permute-done | bytes 131104 | tf_op jit(solution)/shard_map/ppermute | solution.py:239
  18.0 0.1 collective-permute-start.4
  18.1 1.5 %collective-permute-done.4.far_ref = bf16[32,4096]{1,0:T(8,128)(2,1)S(1)} collective-permute-done((bf16[32,4096]{1,0:T(8,128)(2,1)S(1)}, bf16[32,4096]{1,0:T(8,128)(2,1)S(1)}, u32[]{:S(2)}, u32[]{:S(2)}) %collective-permute-start.4) | collective-permute-done | bytes 262176 | tf_op jit(solution)/shard_map/ppermute | solution.py:239
  19.6 1.0 %shard_map.106 = (f32[4,64]{1,0:T(4,128)}, f32[1,64]{1,0:T(1,128)S(1)}) custom-call(s32[1]{0:T(128)} %bitcast.me_ref, bf16[4,4096]{1,0:T(4,128)(2,1)S(1)} %shard_map.105.sk_ref, bf16[32,4096]{1,0:T(8,128)(2,1)S(1)} %pad_maximum_fusion.near_ref, bf16[32,4096]{1,0:T(8,128)(2,1)S(1)} %collective-permute-done.4.far_ref), custom_call_target="tpu_custom_call" | custom-call | flops 2097152 | bytes 524288 | tf_op jit(solution)/shard_map/pallas_call | solution.py:228
  20.6 0.1 slice_bitcast_fusion
  20.7 0.1 collective-permute-start.5
  20.8 1.0 %collective-permute-done.5 = f32[32]{0:T(128)S(1)} collective-permute-done((f32[32]{0:T(128)S(1)}, f32[32]{0:T(128)S(1)}, u32[]{:S(2)}, u32[]{:S(2)}) %collective-permute-start.5) | collective-permute-done | bytes 160 | tf_op jit(solution)/shard_map/ppermute | solution.py:239
  21.8 0.1 slice.35
  21.9 1.7 %collective-permute-start.6 = (f32[16]{0:T(128)S(1)}, f32[16]{0:T(128)S(1)}, u32[]{:S(2)}, u32[]{:S(2)}) collective-permute-start(f32[16]{0:T(128)S(1)} %slice.35), channel_id=1, source_target_pairs={{0,2},{1,3},{2,0},{3,1},{4,6},{5,7},{6,4},{7,5},{8,10},{9,11},{10,... | collective-permute-start | bytes 200 | tf_op jit(solution)/shard_map/ppermute | solution.py:239
  23.6 1.8 %collective-permute-done.6 = f32[16]{0:T(128)S(1)} collective-permute-done((f32[16]{0:T(128)S(1)}, f32[16]{0:T(128)S(1)}, u32[]{:S(2)}, u32[]{:S(2)}) %collective-permute-start.6) | collective-permute-done | bytes 96 | tf_op jit(solution)/shard_map/ppermute | solution.py:239
  25.4 0.1 slice.37
  25.5 0.9 %collective-permute-start.7 = (f32[8]{0:T(128)S(1)}, f32[8]{0:T(128)S(1)}, u32[]{:S(2)}, u32[]{:S(2)}) collective-permute-start(f32[8]{0:T(128)S(1)} %slice.37), channel_id=1, source_target_pairs={{0,4},{1,5},{2,6},{3,7},{4,0},{5,1},{6,2},{7,3},{8,12},{9,13},{10,... | collective-permute-start | bytes 104 | tf_op jit(solution)/shard_map/ppermute | solution.py:239
  26.4 2.6 %collective-permute-done.7 = f32[8]{0:T(128)S(1)} collective-permute-done((f32[8]{0:T(128)S(1)}, f32[8]{0:T(128)S(1)}, u32[]{:S(2)}, u32[]{:S(2)}) %collective-permute-start.7) | collective-permute-done | bytes 64 | tf_op jit(solution)/shard_map/ppermute | solution.py:239
  29.0 0.1 slice.39
  29.1 2.4 %collective-permute-start.8 = (f32[4]{0:T(128)S(1)}, f32[4]{0:T(128)S(1)}, u32[]{:S(2)}, u32[]{:S(2)}) collective-permute-start(f32[4]{0:T(128)S(1)} %slice.39), channel_id=1, source_target_pairs={{0,8},{1,9},{2,10},{3,11},{4,12},{5,13},{6,14},{7,15},{8,0},{9,1},... | collective-permute-start | bytes 56 | tf_op jit(solution)/shard_map/ppermute | solution.py:239
  31.5 2.1 %collective-permute-done.8 = f32[4]{0:T(128)S(1)} collective-permute-done((f32[4]{0:T(128)S(1)}, f32[4]{0:T(128)S(1)}, u32[]{:S(2)}, u32[]{:S(2)}) %collective-permute-start.8) | collective-permute-done | bytes 48 | tf_op jit(solution)/shard_map/ppermute | solution.py:239
  33.6 0.5 %add_multiply_fusion = f32[4]{0:T(128)} fusion(f32[4]{0:T(128)S(1)} %collective-permute-done.8, f32[8]{0:T(128)S(1)} %slice_add_fusion), kind=kLoop, calls=%fused_computation.3 | loop fusion | flops 8 | bytes 48 | tf_op jit(solution)/shard_map/div | solution.py:260
  (4 shorter events, 0.0 us)
Async XLA Ops:
  0.6 12.2 %collective-permute-start.1 = (bf16[4,4096]{1,0:T(4,128)(2,1)}, bf16[4,4096]{1,0:T(4,128)(2,1)S(1)}, u32[]{:S(2)}, u32[]{:S(2)}) collective-permute-start(bf16[4,4096]{1,0:T(4,128)(2,1)} %param.15), channel_id=1, source_target_pairs={{0,4},{1,5},{2,6},{3,7},{4,0},{5,1},{6,2},{7,3},{8,12},{9,13},{10,... | collective-permute-start | bytes 98312 | tf_op jit(solution)/shard_map/ppermute | solution.py:239
  3.7 9.1 %collective-permute-start = (bf16[4,4096]{1,0:T(4,128)(2,1)}, bf16[4,4096]{1,0:T(4,128)(2,1)S(1)}, u32[]{:S(2)}, u32[]{:S(2)}) collective-permute-start(bf16[4,4096]{1,0:T(4,128)(2,1)} %param.15), channel_id=1, source_target_pairs={{0,8},{1,9},{2,10},{3,11},{4,12},{5,13},{6,14},{7,15},{8,0},{9,1},... | collective-permute-start | bytes 98312 | tf_op jit(solution)/shard_map/ppermute | solution.py:239
  6.3 6.5 %collective-permute-start.2 = (bf16[4,4096]{1,0:T(4,128)(2,1)}, bf16[4,4096]{1,0:T(4,128)(2,1)S(1)}, u32[]{:S(2)}, u32[]{:S(2)}) collective-permute-start(bf16[4,4096]{1,0:T(4,128)(2,1)} %param.15), channel_id=1, source_target_pairs={{0,12},{1,13},{2,14},{3,15},{4,8},{5,9},{6,10},{7,11},{8,4},{9,5},... | collective-permute-start | bytes 98312 | tf_op jit(solution)/shard_map/ppermute | solution.py:239
  6.3 6.5 %copy-start.2 = (bf16[4,4096]{1,0:T(4,128)(2,1)S(1)}, bf16[4,4096]{1,0:T(4,128)(2,1)}, u32[]{:S(2)}) copy-start(bf16[4,4096]{1,0:T(4,128)(2,1)} %param.15) | copy-start | bytes 98308
  6.3 8.4 %copy-start = (bf16[1024,512]{1,0:T(8,128)(2,1)S(1)}, bf16[1024,512]{1,0:T(8,128)(2,1)}, u32[]{:S(2)}) copy-start(bf16[1024,512]{1,0:T(8,128)(2,1)} %constant.11.clone.m) | copy-start | bytes 3145732
  12.8 2.0 %copy-start.1 = (f32[24,256]{1,0:T(8,128)S(1)}, f32[24,256]{1,0:T(8,128)}, u32[]{:S(2)}) copy-start(f32[24,256]{1,0:T(8,128)} %constant.12.clone.tw) | copy-start | bytes 73732
  13.0 5.0 %collective-permute-start.3 = (bf16[16,4096]{1,0:T(8,128)(2,1)S(1)}, bf16[16,4096]{1,0:T(8,128)(2,1)S(1)}, u32[]{:S(2)}, u32[]{:S(2)}) collective-permute-start(bf16[16,4096]{1,0:T(8,128)(2,1)S(1)} %pad_maximum_fusion.1), channel_id=1, source_target_pairs={{0,2},{1,3},{2,0},{3,1},{4,6},{5,7},{6,4},{7,5},{8,10},{9,11},{10,... | collective-permute-start | bytes 393224 | tf_op jit(solution)/shard_map/ppermute | solution.py:239
  18.0 1.6 %collective-permute-start.4 = (bf16[32,4096]{1,0:T(8,128)(2,1)S(1)}, bf16[32,4096]{1,0:T(8,128)(2,1)S(1)}, u32[]{:S(2)}, u32[]{:S(2)}) collective-permute-start(bf16[32,4096]{1,0:T(8,128)(2,1)S(1)} %pad_maximum_fusion.near_ref), channel_id=1, source_target_pairs={{0,1},{1,0},{2,3},{3,2},{4,5},{5,4},{6,7},{7,6},{8,9},{9,8},{10,11... | collective-permute-start | bytes 786440 | tf_op jit(solution)/shard_map/ppermute | solution.py:239
  20.7 1.1 %collective-permute-start.5 = (f32[32]{0:T(128)S(1)}, f32[32]{0:T(128)S(1)}, u32[]{:S(2)}, u32[]{:S(2)}) collective-permute-start(f32[32]{0:T(128)S(1)} %slice_bitcast_fusion), channel_id=1, source_target_pairs={{0,1},{1,0},{2,3},{3,2},{4,5},{5,4},{6,7},{7,6},{8,9},{9,8},{10,11... | collective-permute-start | bytes 392 | tf_op jit(solution)/shard_map/ppermute | solution.py:239
  21.9 3.5 %collective-permute-start.6 = (f32[16]{0:T(128)S(1)}, f32[16]{0:T(128)S(1)}, u32[]{:S(2)}, u32[]{:S(2)}) collective-permute-start(f32[16]{0:T(128)S(1)} %slice.35), channel_id=1, source_target_pairs={{0,2},{1,3},{2,0},{3,1},{4,6},{5,7},{6,4},{7,5},{8,10},{9,11},{10,... | collective-permute-start | bytes 200 | tf_op jit(solution)/shard_map/ppermute | solution.py:239
  25.5 3.5 %collective-permute-start.7 = (f32[8]{0:T(128)S(1)}, f32[8]{0:T(128)S(1)}, u32[]{:S(2)}, u32[]{:S(2)}) collective-permute-start(f32[8]{0:T(128)S(1)} %slice.37), channel_id=1, source_target_pairs={{0,4},{1,5},{2,6},{3,7},{4,0},{5,1},{6,2},{7,3},{8,12},{9,13},{10,... | collective-permute-start | bytes 104 | tf_op jit(solution)/shard_map/ppermute | solution.py:239
  29.1 4.4 %collective-permute-start.8 = (f32[4]{0:T(128)S(1)}, f32[4]{0:T(128)S(1)}, u32[]{:S(2)}, u32[]{:S(2)}) collective-permute-start(f32[4]{0:T(128)S(1)} %slice.39), channel_id=1, source_target_pairs={{0,8},{1,9},{2,10},{3,11},{4,12},{5,13},{6,14},{7,15},{8,0},{9,1},... | collective-permute-start | bytes 56 | tf_op jit(solution)/shard_map/ppermute | solution.py:239

commit v3 on v2

v3 whole, which is shorter than its diff:
```python
import functools, math
import numpy as np
import jax, jax.numpy as jnp
from jax import lax
from jax.experimental import pallas as pl
from jax.experimental.pallas import tpu as pltpu
from jax.sharding import PartitionSpec as P

bf = jnp.bfloat16
f32 = jnp.float32
NT = (((1,), (1,)), ((), ()))
VMEM_LIMIT = 24 << 20
RADIX = 16


def rfft(x):
    n=len(x)
    if n==1: return [(x[0],None)]
    if n==2: return [(x[0]+x[1],None),(x[0]-x[1],None)]
    e=rfft(x[0::2]); o=rfft(x[1::2]); h=n//2; out=[None]*(h+1)
    out[0]=(e[0][0]+o[0][0],None); out[h]=(e[0][0]-o[0][0],None)
    for k in range(1,h//2):
        c,s=math.cos(2*math.pi*k/n),math.sin(2*math.pi*k/n)
        re,im=o[k]
        if 8*k==n:
            tr=(re+im)*c; ti=(im-re)*c
        else:
            tr=re*c+im*s; ti=im*c-re*s
        out[k]=(e[k][0]+tr,e[k][1]+ti); out[h-k]=(e[k][0]-tr,ti-e[k][1])
    out[h//2]=(e[h//2][0],-o[h//2][0])
    return out

def irfft(X):
    h=len(X)-1; n=2*h
    if h==0: return [X[0][0]]
    if h==1: return [X[0][0]+X[1][0],X[0][0]-X[1][0]]
    E=[None]*(h//2+1); O=[None]*(h//2+1)
    E[0]=(X[0][0]+X[h][0],None); O[0]=(X[0][0]-X[h][0],None)
    for k in range(1,h//2):
        c,s=math.cos(2*math.pi*k/n),math.sin(2*math.pi*k/n)
        (ar,ai),(br,bi)=X[k],X[h-k]
        E[k]=(ar+br,ai-bi)
        dr,di=ar-br,ai+bi
        if 8*k==n: O[k]=((dr-di)*c,(dr+di)*c)
        else: O[k]=(dr*c-di*s,dr*s+di*c)
    r,i=X[h//2]
    E[h//2]=(2.0*r,None); O[h//2]=(-2.0*i,None)
    ev=irfft(E); od=irfft(O); out=[None]*n
    out[0::2]=ev; out[1::2]=od
    return out


def tables(A, W):
    i = np.arange(W)
    ang = 2 * np.pi * (np.outer(i, i) % W) / W
    c, s = np.cos(ang), np.sin(ang)
    m = np.block([[c, -s], [s, c]]).astype(np.float32)
    hi = m.astype(jnp.bfloat16)
    lo = (m - hi.astype(np.float32)).astype(jnp.bfloat16)
    t = 2 * np.pi * np.outer(np.arange(A // 2 + 1), i) / (A * W)
    tw = np.concatenate([np.cos(t), np.sin(t)], 0).astype(np.float32)
    tw = np.concatenate([tw, np.zeros((-len(tw) % 8, W), np.float32)], 0)
    return np.concatenate([hi, lo], 0), tw


def split(z):
    hi = z.astype(bf)
    return hi, (z - hi.astype(f32)).astype(bf)


def onehot(h_ref, bt, W):
    it = lax.broadcasted_iota(jnp.int32, (W, 128), 0).astype(f32).astype(bf)
    one, zero = jnp.ones((W, 128), bf), jnp.zeros((W, 128), bf)
    for j in range(h_ref.shape[0]):
        b = (h_ref[j : j + 1, :] & (W - 1)).astype(f32).astype(bf)
        bt[:, j * 128 : (j + 1) * 128] = jnp.where(it == jnp.broadcast_to(b, (W, 128)), one, zero)


def count(x, h_ref, s_ref, bt, A, W):
    cols = []
    for j in range(h_ref.shape[0]):
        sg = (2 * s_ref[j : j + 1, :] - 1).astype(f32).astype(bf)
        a = lax.shift_right_logical(h_ref[j : j + 1, :], W.bit_length() - 1).astype(f32).astype(bf)
        xs = x[:, j * 128 : (j + 1) * 128] * sg
        ab = jnp.broadcast_to(a, xs.shape)
        z = jnp.zeros_like(xs)
        cols.append(jnp.concatenate([jnp.where(ab == jnp.asarray(k, bf), xs, z) for k in range(A)], 0))
    return lax.dot_general(jnp.concatenate(cols, 1), bt[...], NT, preferred_element_type=f32)


def class_rows(cnt, base, R, q, T, tw, z, row0, A, W):
    H = A // 2 + 1
    for t in range(0, T, 8):
        for l in range(0, W, 128):
            starts = [base + k * R + q * T + t for k in range(A)]
            planes = [cnt[i : i + 8, l : l + 128] for i in starts]
            for n, (re, im) in enumerate(rfft(planes)):
                if n:
                    c, s = tw[n : n + 1, l : l + 128], tw[H + n : H + n + 1, l : l + 128]
                    re, im = (re * c, -re * s) if im is None else (re * c + im * s, im * c - re * s)
                else:
                    im = jnp.zeros_like(re)
                r = slice(row0 + n * T + t, row0 + n * T + t + 8)
                z[r, l : l + 128] = re
                z[r, W + l : W + l + 128] = im


def dft(z, m, W):
    hi, lo = split(z)
    lhs = jnp.concatenate([hi, lo, hi], 1)
    out = []
    for o in (0, W):
        m_hi, m_lo = m[: 2 * W, o : o + W], m[2 * W :, o : o + W]
        out.append(jnp.dot(lhs, jnp.concatenate([m_hi, m_hi, m_lo], 0), preferred_element_type=f32))
    return out


def first_kernel(*refs, A, W):
    given, (cx, y, ho, so, x, hi, si, bt, sem) = refs[:6], refs[6:]
    copies = [pltpu.make_async_copy(a, b, sem.at[i]) for i, (a, b) in enumerate(zip(given, (hi, si, x, ho, so, y)))]
    for c in copies:
        c.start()
    for c in copies:
        c.wait()
    onehot(hi, bt, W)
    cx[...] = count(x, hi, si, bt, A, W)


def second_kernel(cx, y, ho, so, m, tw, out, zx, bt, *, Q, T, A, W):
    H, R = A // 2 + 1, Q * T
    for q in range(Q):
        class_rows(cx, 0, R, q, T, tw, zx, q * H * T, A, W)
    out[: H * R, :], out[H * R : 2 * H * R, :] = dft(zx[...], m, W)
    onehot(ho, bt, W)
    out[2 * H * R :, :] = count(y, ho, so, bt, A, W)


def third_kernel(f, m, tw, o_ref, zy, p, *, Q, T, A, W):
    H, R = A // 2 + 1, Q * T
    p[...] = jnp.zeros_like(p)
    for q in range(Q):
        class_rows(f, 2 * H * R, R, q, T, tw, zy, q * H * T, A, W)
    re, im = dft(zy[...], m, W)
    for q in range(Q):
        here = lax.broadcasted_iota(jnp.int32, (8, W), 0) == q
        for k in range(H):
            a = slice((q * H + k) * T, (q * H + k + 1) * T)
            fr, fi = f[a, :], f[H * R + a.start : H * R + a.stop, :]
            pr = jnp.sum(fr * re[a] - fi * im[a], 0, keepdims=True)
            pi = jnp.sum(fr * im[a] + fi * re[a], 0, keepdims=True)
            r = slice(8 * k, 8 * k + 8)
            p[r, :W] = jnp.where(here, jnp.broadcast_to(pr, (8, W)), p[r, :W])
            p[r, W:] = jnp.where(here, jnp.broadcast_to(pi, (8, W)), p[r, W:])
    for k, v in enumerate(back(p[...], m, tw, A, W)):
        o_ref[:, k * W : (k + 1) * W] = v[:Q].astype(o_ref.dtype)


def back(p, m, tw, A, W):
    H = A // 2 + 1
    scale = 1.0 / (A * W)
    re_all, im_all = dft(p * jnp.where(lax.broadcasted_iota(jnp.int32, p.shape, 1) < W, scale, -scale), m, W)
    X = []
    for k in range(H):
        re, im = re_all[8 * k : 8 * k + 8], -im_all[8 * k : 8 * k + 8]
        if k == 0:
            X.append((re, None))
            continue
        c, s = tw[k : k + 1, :], tw[H + k : H + k + 1, :]
        X.append((re * c - im * s, None if k == A // 2 else re * s + im * c))
    return irfft(X)


def call(kernel, out, args, scratch, flops, spec=pltpu.VMEM):
    vm = pl.BlockSpec(memory_space=pltpu.VMEM)
    return pl.pallas_call(
        kernel,
        out_shape=out,
        in_specs=[pl.BlockSpec(memory_space=spec)] * len(args),
        out_specs=jax.tree.map(lambda _: vm, out),
        scratch_shapes=scratch,
        cost_estimate=pl.CostEstimate(flops=flops, bytes_accessed=4 << 20, transcendentals=0),
        compiler_params=pltpu.CompilerParams(vmem_limit_bytes=VMEM_LIMIT),
    )(*args)


def first(x, y, hi, si, ho, so, A, W):
    R, D = x.shape
    like = lambda v: jax.ShapeDtypeStruct(v.shape, v.dtype)
    args = [pltpu.with_memory_space_constraint(v, pltpu.HBM) for v in (hi, si, x, ho, so, y)]
    scratch = [pltpu.VMEM(v.shape, v.dtype) for v in (x, hi, si)] + [pltpu.VMEM((W, D), bf), pltpu.SemaphoreType.DMA((6,))]
    out = (jax.ShapeDtypeStruct((A * R, W), f32), like(y), like(ho), like(so))
    return call(functools.partial(first_kernel, A=A, W=W), out, args, scratch, 2 * R * D * A * W, pltpu.HBM)


def second(cx, y, ho, so, m, tw, Q, A):
    W = cx.shape[1]
    R = cx.shape[0] // A
    rows = R * (A // 2 + 1)
    out = jax.ShapeDtypeStruct((2 * rows + A * R, W), f32)
    scratch = [pltpu.VMEM((rows, 2 * W), f32), pltpu.VMEM((W, y.shape[1]), bf)]
    return call(functools.partial(second_kernel, Q=Q, T=R // Q, A=A, W=W), out, (cx, y, ho, so, m, tw), scratch, 2 * R * y.shape[1] * A * W)


def third(f, m, tw, Q, R, A):
    W, H = f.shape[1], A // 2 + 1
    assert Q <= 8
    out = jax.ShapeDtypeStruct((Q, A * W), bf)
    scratch = [pltpu.VMEM((R * H, 2 * W), f32), pltpu.VMEM((H * 8, 2 * W), f32)]
    return call(functools.partial(third_kernel, Q=Q, T=R // Q, A=A, W=W), out, (f, m, tw), scratch, 1 << 31)


def score_kernel(me_ref, sk_ref, *refs, bits, e, n):
    parts, (s_ref, t_ref) = refs[:-2], refs[-2:]
    rows = jnp.concatenate([r[...] for r in parts], 0)
    s = lax.dot_general(sk_ref[...], rows, NT, preferred_element_type=f32)
    count = n * e
    shift = e.bit_length() - 1

    def device_of(p):
        device = jnp.broadcast_to(me_ref[0], p.shape)
        for i, bit in enumerate(bits):
            device = device ^ (((p >> (shift + i)) & 1) * bit)
        return device

    def thirds(v):
        hi = v.astype(bf)
        rest = v - hi.astype(f32)
        mid = rest.astype(bf)
        return hi, mid, (rest - mid.astype(f32)).astype(bf)

    def pick(v, m):
        hi, mid, low = (jnp.dot(u, m, preferred_element_type=f32) for u in thirds(v))
        return hi + (mid + low)

    def ones_where(m):
        return jnp.where(m, 1.0, 0.0).astype(bf)

    def iota(shape, d):
        return lax.broadcasted_iota(jnp.int32, shape, d)

    p = iota((count, count), 0)
    place = (device_of(p) << shift) | (p & (e - 1))
    s_ref[...] = pick(s, ones_where(place == iota((count, count), 1)))
    sums = jnp.broadcast_to(jnp.sum(s, 0, keepdims=True), (n, count))
    mine = jnp.where(device_of(iota((n, count), 1)) == iota((n, count), 0), sums, 0.0)
    t_ref[...] = pick(mine, ones_where((iota((count, e), 0) & (e - 1)) == iota((count, e), 1)))


def score(me, sk, parts, bits, n):
    q, total = sk.shape[0], sum(v.shape[0] for v in parts)
    e = total // n
    assert e & (e - 1) == 0
    vm = pl.BlockSpec(memory_space=pltpu.VMEM)
    return pl.pallas_call(
        functools.partial(score_kernel, bits=bits, e=e, n=n),
        out_shape=(jax.ShapeDtypeStruct((q, total), f32), jax.ShapeDtypeStruct((n, e), f32)),
        in_specs=[pl.BlockSpec(memory_space=pltpu.SMEM)] + [vm] * (1 + len(parts)),
        out_specs=(vm, vm),
        cost_estimate=pl.CostEstimate(flops=2 * q * total * sk.shape[1], bytes_accessed=total * 8192, transcendentals=0),
        compiler_params=pltpu.CompilerParams(vmem_limit_bytes=16 << 20),
    )(me.reshape(1), sk, *parts)


def swap(v, bit, n):
    return lax.ppermute(v, "store", [(i, i ^ bit) for i in range(n)])


def body(query_inputs, query_grads, hash_in, sign_in, hash_out, sign_out, stored):
    n = lax.axis_size("store")
    q_dev, e = query_inputs.shape[0], stored.shape[0]
    bits = [1 << b for b in reversed(range(n.bit_length() - 1))]
    b0, b1 = bits[:2]
    parts = [stored] + [swap(stored, bit, n) for bit in (b0, b1, b0 ^ b1)]
    A, width = RADIX, stored.shape[1]
    m, tw = (jnp.asarray(v) for v in tables(A, width // A))
    tokens = q_dev * query_inputs.shape[1]
    tabs = (v.reshape(-1, 128) for v in (hash_in, sign_in, hash_out, sign_out))
    cx, *rest = first(query_inputs.reshape(tokens, -1), query_grads.reshape(tokens, -1), *tabs, A, width // A)
    rows, cx = lax.optimization_barrier((jnp.concatenate(parts, 0), cx))
    for bit in bits[2:-2]:
        rows = jnp.concatenate([rows, swap(rows, bit, n)], 0)
    across = swap(rows, bits[-2], n)
    twin = swap(rows, bits[-1], n)
    f = second(cx, *rest, m, tw, q_dev, A)
    across, f = lax.optimization_barrier((across, f))
    twin_across = swap(across, bits[-1], n)
    sk = third(f, m, tw, q_dev, tokens, A)
    scores, t = score(lax.axis_index("store"), sk, [rows, across, twin, twin_across], bits, n)
    totals = jnp.sum(lax.all_to_all(t, "store", 0, 0), 0)
    return scores, totals / (n * q_dev)


def solution(mesh):
    rows = P(("grp", "store"), None)
    cube = P(("grp", "store"), None, None)
    return jax.shard_map(
        body,
        mesh=mesh,
        in_specs=(cube, cube, P(), P(), P(), P(), rows),
        out_specs=(rows, P(("grp", "store"))),
        check_vma=False,
    )
```

time: 34.2 us -> 31.4 us (0.918)
  blocking collectives: 0 us -> 9.95 us
  waiting for transfers between devices: 9.51 us -> 1.91 us
  starting transfers between devices: 12.7 us -> 7.83 us
    all_to_all x0 -> x1, blocking collectives: none -> 9.95 us  [body(): totals = jnp.sum(lax.all_to_all(t, 'store', 0, 0), 0)]
    ppermute x9 -> x6, waiting for transfers between devices: 9.51 us -> 1.91 us  [swap(): return lax.ppermute(v, 'store', [(i, i ^ bit) for i in range(n)])]
    ppermute x9 -> x6, starting transfers between devices: 12.7 us -> 7.83 us  [swap(): return lax.ppermute(v, 'store', [(i, i ^ bit) for i in range(n)])]
    pallas_call x3 -> x4, Pallas kernels: 10.2 us -> 10.2 us  [the longest x3 9.18 us: call(): pl.pallas_call(kernel, out_shape=out, in_specs=[pl.BlockSpec(memory_space...]
  transfers between devices with their start and end apart: 9 -> 6, of which waited for: 6 -> 1; matrix products, arithmetic and copies ran while one was open for 0% -> 0% of each run, Pallas kernels for 27% -> 29%
where the time goes in v3:
time: 31.4 us; the launch traced here: 31.2 us
  Pallas kernels  10.2 us (32%)
  blocking collectives  9.95 us (32%)
  starting transfers between devices  7.83 us (25%)
  waiting for transfers between devices  1.91 us (6%)
  between operations  0.72 us (2%)
  other arithmetic  0.63 us (2%)
    all_to_all x1, blocking collectives, body(): totals = jnp.sum(lax.all_to_all(t, 'store', 0, 0), 0)  9.95 us
    pallas_call x3, Pallas kernels, call(): pl.pallas_call(kernel, out_shape=out, in_specs=[pl.BlockSpec(memory_space...  9.18 us
    ppermute x6, starting transfers between devices, swap(): return lax.ppermute(v, 'store', [(i, i ^ bit) for i in range(n)])  7.83 us
    ppermute x6, waiting for transfers between devices, swap(): return lax.ppermute(v, 'store', [(i, i ^ bit) for i in range(n)])  1.91 us
    pallas_call x1, Pallas kernels, score(): pl.pallas_call(functools.partial(score_kernel, bits=bits, e=e, n=n), out_...  1 us
  transfers between devices with their start and end apart: 6, of which 1 were waited for; matrix products, arithmetic and copies ran while one was open for 0% of the time, Pallas kernels for 29%

profile of v3, /device:TPU:0, one launch (start us, length us, event | category | flops | bytes accessed | tf_op | source)
XLA Modules:
  0.0 31.2 jit_solution(15107155166776836936)
XLA Ops:
  0.6 4.1 %collective-permute-start = (bf16[4,4096]{1,0:T(4,128)(2,1)}, bf16[4,4096]{1,0:T(4,128)(2,1)S(1)}, u32[]{:S(2)}, u32[]{:S(2)}) collective-permute-start(bf16[4,4096]{1,0:T(4,128)(2,1)} %param.15), channel_id=1, source_target_pairs={{0,8},{1,9},{2,10},{3,11},{4,12},{5,13},{6,14},{7,15},{8,0},{9,1},... | collective-permute-start | bytes 98312 | tf_op jit(solution)/shard_map/ppermute | solution.py:265
  4.7 1.6 %collective-permute-start.1 = (bf16[4,4096]{1,0:T(4,128)(2,1)}, bf16[4,4096]{1,0:T(4,128)(2,1)S(1)}, u32[]{:S(2)}, u32[]{:S(2)}) collective-permute-start(bf16[4,4096]{1,0:T(4,128)(2,1)} %param.15), channel_id=1, source_target_pairs={{0,4},{1,5},{2,6},{3,7},{4,0},{5,1},{6,2},{7,3},{8,12},{9,13},{10,... | collective-permute-start | bytes 98312 | tf_op jit(solution)/shard_map/ppermute | solution.py:265
  6.3 0.0 collective-permute-start.2
  6.3 0.0 copy-start.2
  6.3 0.0 copy-start
  6.3 0.0 copy-start.1
  6.3 4.0 %shard_map.104 = (f32[1024,256]{1,0:T(8,128)S(1)}, bf16[64,4096]{1,0:T(8,128)(2,1)S(1)}, s32[32,128]{1,0:T(8,128)S(1)}, s32[32,128]{1,0:T(8,128)S(1)}) custom-call(s32[32,128]{1,0:T(8,128)} %bitcast.13, s32[32,128]{1,0:T(8,128)} %bitcast.14, bf16[64,4096]{1,0:T(8,128)(2,1)} %bitcast.11, s32[32,128]{1,0:T(8,128)} %bitcast.15, s32[32,128]{1,0:T(8,128)} %bitcast.16, ...), custom_call_target="tpu_custom_call" | custom-call | flops 2147483648 | bytes 4194304 | tf_op jit(solution)/shard_map/pallas_call | solution.py:175
  10.3 0.0 collective-permute-done
  10.3 0.0 collective-permute-done.1
  10.3 1.9 %collective-permute-done.2 = bf16[4,4096]{1,0:T(4,128)(2,1)S(1)} collective-permute-done((bf16[4,4096]{1,0:T(4,128)(2,1)}, bf16[4,4096]{1,0:T(4,128)(2,1)S(1)}, u32[]{:S(2)}, u32[]{:S(2)}) %collective-permute-start.2) | collective-permute-done | bytes 32800 | tf_op jit(solution)/shard_map/ppermute | solution.py:265
  12.2 0.0 copy-done.2
  12.2 0.1 pad_maximum_fusion.refs_0_
  12.3 1.6 %collective-permute-start.3 = (bf16[16,4096]{1,0:T(8,128)(2,1)S(1)}, bf16[16,4096]{1,0:T(8,128)(2,1)S(1)}, u32[]{:S(2)}, u32[]{:S(2)}) collective-permute-start(bf16[16,4096]{1,0:T(8,128)(2,1)S(1)} %pad_maximum_fusion.refs_0_), channel_id=1, source_target_pairs={{0,2},{1,3},{2,0},{3,1},{4,6},{5,7},{6,4},{7,5},{8,10},{9,11},{10,... | collective-permute-start | bytes 393224 | tf_op jit(solution)/shard_map/ppermute | solution.py:265
  13.9 0.0 collective-permute-start.4
  13.9 0.0 copy-done
  13.9 0.0 copy-done.1
  13.9 3.5 %shard_map.105.f = f32[2176,256]{1,0:T(8,128)S(1)} custom-call(f32[1024,256]{1,0:T(8,128)S(1)} %get-tuple-element.14.cx, bf16[64,4096]{1,0:T(8,128)(2,1)S(1)} %get-tuple-element.15.y, s32[32,128]{1,0:T(8,128)S(1)} %get-tuple-element.16.ho, s32[32,128]{1,0:T(8,128)S(1)} %get-tuple-element.17.so, bf16[1024,512]{1,0:T(8,128)(2,1)S(1)} %copy-done, ...), custom_call_target="tpu_custom_call" | custom-call | flops 2147483648 | bytes 4194304 | tf_op jit(solution)/shard_map/pallas_call | solution.py:175
  17.4 0.0 collective-permute-done.3.refs_1_
  17.4 0.6 %collective-permute-start.5 = (bf16[16,4096]{1,0:T(8,128)(2,1)S(1)}, bf16[16,4096]{1,0:T(8,128)(2,1)S(1)}, u32[]{:S(2)}, u32[]{:S(2)}) collective-permute-start(bf16[16,4096]{1,0:T(8,128)(2,1)S(1)} %collective-permute-done.3.refs_1_), channel_id=1, source_target_pairs={{0,1},{1,0},{2,3},{3,2},{4,5},{5,4},{6,7},{7,6},{8,9},{9,8},{10,11... | collective-permute-start | bytes 393224 | tf_op jit(solution)/shard_map/ppermute | solution.py:265
  18.0 1.7 %shard_map.106.sk_ref = bf16[4,4096]{1,0:T(4,128)(2,1)S(1)} custom-call(f32[2176,256]{1,0:T(8,128)S(1)} %shard_map.105.f, bf16[1024,512]{1,0:T(8,128)(2,1)S(1)} %copy-done, f32[24,256]{1,0:T(8,128)S(1)} %copy-done.1), custom_call_target="tpu_custom_call" | custom-call | flops 2147483648 | bytes 4194304 | tf_op jit(solution)/shard_map/pallas_call | solution.py:175
  19.7 0.0 collective-permute-done.4.refs_2_
  19.7 0.0 collective-permute-done.5.refs_3_
  19.7 1.0 %shard_map.107 = (f32[4,64]{1,0:T(4,128)}, f32[16,4]{1,0:T(8,128)S(1)}) custom-call(s32[1]{0:T(128)} %bitcast.me_ref, bf16[4,4096]{1,0:T(4,128)(2,1)S(1)} %shard_map.106.sk_ref, bf16[16,4096]{1,0:T(8,128)(2,1)S(1)} %pad_maximum_fusion.refs_0_, bf16[16,4096]{1,0:T(8,128)(2,1)S(1)} %collective-permute-done.3.refs_1_, ...), custom_call_target="tpu_custom_call" | custom-call | flops 2097152 | bytes 524288 | tf_op jit(solution)/shard_map/pallas_call | solution.py:254
  20.7 9.9 %all_to_all.9 = f32[16,1,4]{2,1,0:T(1,128)S(1)} all-to-all(f32[16,1,4]{2,1,0:T(1,128)S(1)} %bitcast.10), channel_id=1, replica_groups=mesh['grp'=2,'store'=16] {'store'}, dimensions={0} | all-to-all | bytes 512 | tf_op jit(solution)/shard_map/all_to_all | solution.py:289
  30.7 0.5 %broadcast_multiply_fusion = f32[4]{0:T(128)} fusion(f32[4]{0:T(128)S(1)} %reduce_sum.9), kind=kLoop, calls=%fused_computation.1 | loop fusion | flops 4 | bytes 32 | tf_op jit(solution)/shard_map/div | solution.py:290
  (1 shorter events, 0.0 us)
Async XLA Ops:
  0.6 9.7 %collective-permute-start = (bf16[4,4096]{1,0:T(4,128)(2,1)}, bf16[4,4096]{1,0:T(4,128)(2,1)S(1)}, u32[]{:S(2)}, u32[]{:S(2)}) collective-permute-start(bf16[4,4096]{1,0:T(4,128)(2,1)} %param.15), channel_id=1, source_target_pairs={{0,8},{1,9},{2,10},{3,11},{4,12},{5,13},{6,14},{7,15},{8,0},{9,1},... | collective-permute-start | bytes 98312 | tf_op jit(solution)/shard_map/ppermute | solution.py:265
  4.7 5.6 %collective-permute-start.1 = (bf16[4,4096]{1,0:T(4,128)(2,1)}, bf16[4,4096]{1,0:T(4,128)(2,1)S(1)}, u32[]{:S(2)}, u32[]{:S(2)}) collective-permute-start(bf16[4,4096]{1,0:T(4,128)(2,1)} %param.15), channel_id=1, source_target_pairs={{0,4},{1,5},{2,6},{3,7},{4,0},{5,1},{6,2},{7,3},{8,12},{9,13},{10,... | collective-permute-start | bytes 98312 | tf_op jit(solution)/shard_map/ppermute | solution.py:265
  6.3 5.9 %collective-permute-start.2 = (bf16[4,4096]{1,0:T(4,128)(2,1)}, bf16[4,4096]{1,0:T(4,128)(2,1)S(1)}, u32[]{:S(2)}, u32[]{:S(2)}) collective-permute-start(bf16[4,4096]{1,0:T(4,128)(2,1)} %param.15), channel_id=1, source_target_pairs={{0,12},{1,13},{2,14},{3,15},{4,8},{5,9},{6,10},{7,11},{8,4},{9,5},... | collective-permute-start | bytes 98312 | tf_op jit(solution)/shard_map/ppermute | solution.py:265
  6.3 5.9 %copy-start.2 = (bf16[4,4096]{1,0:T(4,128)(2,1)S(1)}, bf16[4,4096]{1,0:T(4,128)(2,1)}, u32[]{:S(2)}) copy-start(bf16[4,4096]{1,0:T(4,128)(2,1)} %param.15) | copy-start | bytes 98308
  6.3 7.6 %copy-start = (bf16[1024,512]{1,0:T(8,128)(2,1)S(1)}, bf16[1024,512]{1,0:T(8,128)(2,1)}, u32[]{:S(2)}) copy-start(bf16[1024,512]{1,0:T(8,128)(2,1)} %constant.13.clone.m) | copy-start | bytes 3145732
  6.3 7.6 %copy-start.1 = (f32[24,256]{1,0:T(8,128)S(1)}, f32[24,256]{1,0:T(8,128)}, u32[]{:S(2)}) copy-start(f32[24,256]{1,0:T(8,128)} %constant.14.clone.tw) | copy-start | bytes 73732
  12.3 5.1 %collective-permute-start.3 = (bf16[16,4096]{1,0:T(8,128)(2,1)S(1)}, bf16[16,4096]{1,0:T(8,128)(2,1)S(1)}, u32[]{:S(2)}, u32[]{:S(2)}) collective-permute-start(bf16[16,4096]{1,0:T(8,128)(2,1)S(1)} %pad_maximum_fusion.refs_0_), channel_id=1, source_target_pairs={{0,2},{1,3},{2,0},{3,1},{4,6},{5,7},{6,4},{7,5},{8,10},{9,11},{10,... | collective-permute-start | bytes 393224 | tf_op jit(solution)/shard_map/ppermute | solution.py:265
  13.9 5.8 %collective-permute-start.4 = (bf16[16,4096]{1,0:T(8,128)(2,1)S(1)}, bf16[16,4096]{1,0:T(8,128)(2,1)S(1)}, u32[]{:S(2)}, u32[]{:S(2)}) collective-permute-start(bf16[16,4096]{1,0:T(8,128)(2,1)S(1)} %pad_maximum_fusion.refs_0_), channel_id=1, source_target_pairs={{0,1},{1,0},{2,3},{3,2},{4,5},{5,4},{6,7},{7,6},{8,9},{9,8},{10,11... | collective-permute-start | bytes 393224 | tf_op jit(solution)/shard_map/ppermute | solution.py:265
  17.4 2.3 %collective-permute-start.5 = (bf16[16,4096]{1,0:T(8,128)(2,1)S(1)}, bf16[16,4096]{1,0:T(8,128)(2,1)S(1)}, u32[]{:S(2)}, u32[]{:S(2)}) collective-permute-start(bf16[16,4096]{1,0:T(8,128)(2,1)S(1)} %collective-permute-done.3.refs_1_), channel_id=1, source_target_pairs={{0,1},{1,0},{2,3},{3,2},{4,5},{5,4},{6,7},{7,6},{8,9},{9,8},{10,11... | collective-permute-start | bytes 393224 | tf_op jit(solution)/shard_map/ppermute | solution.py:265

commit v4 on v3

--- a/solution.py
+++ b/solution.py
@@ -120,34 +120,36 @@
     copies = [pltpu.make_async_copy(a, b, sem.at[i]) for i, (a, b) in enumerate(zip(given, (hi, si, x, ho, so, y)))]
     for c in copies:
         c.start()
-    for c in copies:
+    for c in copies[:3]:
         c.wait()
     onehot(hi, bt, W)
     cx[...] = count(x, hi, si, bt, A, W)
-
-
-def second_kernel(cx, y, ho, so, m, tw, out, zx, bt, *, Q, T, A, W):
+    for c in copies[3:]:
+        c.wait()
+
+
+def second_kernel(cx, y, ho, so, m, tw, fr, fi, zy, zx, cy, bt, *, Q, T, A, W):
     H, R = A // 2 + 1, Q * T
     for q in range(Q):
         class_rows(cx, 0, R, q, T, tw, zx, q * H * T, A, W)
-    out[: H * R, :], out[H * R : 2 * H * R, :] = dft(zx[...], m, W)
     onehot(ho, bt, W)
-    out[2 * H * R :, :] = count(y, ho, so, bt, A, W)
-
-
-def third_kernel(f, m, tw, o_ref, zy, p, *, Q, T, A, W):
-    H, R = A // 2 + 1, Q * T
+    cy[...] = count(y, ho, so, bt, A, W)
+    for q in range(Q):
+        class_rows(cy, 0, R, q, T, tw, zy, q * H * T, A, W)
+    fr[...], fi[...] = dft(zx[...], m, W)
+
+
+def third_kernel(fr, fi, zy, m, tw, o_ref, p, *, Q, T, A, W):
+    H = A // 2 + 1
     p[...] = jnp.zeros_like(p)
-    for q in range(Q):
-        class_rows(f, 2 * H * R, R, q, T, tw, zy, q * H * T, A, W)
     re, im = dft(zy[...], m, W)
     for q in range(Q):
         here = lax.broadcasted_iota(jnp.int32, (8, W), 0) == q
         for k in range(H):
             a = slice((q * H + k) * T, (q * H + k + 1) * T)
-            fr, fi = f[a, :], f[H * R + a.start : H * R + a.stop, :]
-            pr = jnp.sum(fr * re[a] - fi * im[a], 0, keepdims=True)
-            pi = jnp.sum(fr * im[a] + fi * re[a], 0, keepdims=True)
+            ar, ai = fr[a, :], fi[a, :]
+            pr = jnp.sum(ar * re[a] - ai * im[a], 0, keepdims=True)
+            pi = jnp.sum(ar * im[a] + ai * re[a], 0, keepdims=True)
             r = slice(8 * k, 8 * k + 8)
             p[r, :W] = jnp.where(here, jnp.broadcast_to(pr, (8, W)), p[r, :W])
             p[r, W:] = jnp.where(here, jnp.broadcast_to(pi, (8, W)), p[r, W:])
@@ -196,17 +198,16 @@
     W = cx.shape[1]
     R = cx.shape[0] // A
     rows = R * (A // 2 + 1)
-    out = jax.ShapeDtypeStruct((2 * rows + A * R, W), f32)
-    scratch = [pltpu.VMEM((rows, 2 * W), f32), pltpu.VMEM((W, y.shape[1]), bf)]
+    out = (jax.ShapeDtypeStruct((rows, W), f32),) * 2 + (jax.ShapeDtypeStruct((rows, 2 * W), f32),)
+    scratch = [pltpu.VMEM((rows, 2 * W), f32), pltpu.VMEM(cx.shape, f32), pltpu.VMEM((W, y.shape[1]), bf)]
     return call(functools.partial(second_kernel, Q=Q, T=R // Q, A=A, W=W), out, (cx, y, ho, so, m, tw), scratch, 2 * R * y.shape[1] * A * W)
 
 
-def third(f, m, tw, Q, R, A):
-    W, H = f.shape[1], A // 2 + 1
+def third(fr, fi, zy, m, tw, Q, R, A):
+    W, H = fr.shape[1], A // 2 + 1
     assert Q <= 8
     out = jax.ShapeDtypeStruct((Q, A * W), bf)
-    scratch = [pltpu.VMEM((R * H, 2 * W), f32), pltpu.VMEM((H * 8, 2 * W), f32)]
-    return call(functools.partial(third_kernel, Q=Q, T=R // Q, A=A, W=W), out, (f, m, tw), scratch, 1 << 31)
+    return call(functools.partial(third_kernel, Q=Q, T=R // Q, A=A, W=W), out, (fr, fi, zy, m, tw), [pltpu.VMEM((H * 8, 2 * W), f32)], 1 << 31)
 
 
 def score_kernel(me_ref, sk_ref, *refs, bits, e, n):
@@ -217,9 +218,10 @@
     shift = e.bit_length() - 1
 
     def device_of(p):
-        device = jnp.broadcast_to(me_ref[0], p.shape)
-        for i, bit in enumerate(bits):
-            device = device ^ (((p >> (shift + i)) & 1) * bit)
+        block = p >> shift
+        device = (me_ref[0] - (block & 3) * (n // 4)) & (n - 1)
+        for i, bit in enumerate(bits[2:], 2):
+            device = device ^ (((block >> i) & 1) * bit)
         return device
 
     def thirds(v):
@@ -265,12 +267,16 @@
     return lax.ppermute(v, "store", [(i, i ^ bit) for i in range(n)])
 
 
+def turn(v, step, n):
+    return lax.ppermute(v, "store", [(i, (i + step) % n) for i in range(n)])
+
+
 def body(query_inputs, query_grads, hash_in, sign_in, hash_out, sign_out, stored):
     n = lax.axis_size("store")
     q_dev, e = query_inputs.shape[0], stored.shape[0]
     bits = [1 << b for b in reversed(range(n.bit_length() - 1))]
-    b0, b1 = bits[:2]
-    parts = [stored] + [swap(stored, bit, n) for bit in (b0, b1, b0 ^ b1)]
+    parts = [turn(stored, k * n // 4, n) for k in (3, 2, 1)]
+    parts = [stored] + parts[::-1]
     A, width = RADIX, stored.shape[1]
     m, tw = (jnp.asarray(v) for v in tables(A, width // A))
     tokens = q_dev * query_inputs.shape[1]
@@ -281,10 +287,10 @@
         rows = jnp.concatenate([rows, swap(rows, bit, n)], 0)
     across = swap(rows, bits[-2], n)
     twin = swap(rows, bits[-1], n)
-    f = second(cx, *rest, m, tw, q_dev, A)
-    across, f = lax.optimization_barrier((across, f))
+    fr, fi, zy = second(cx, *rest, m, tw, q_dev, A)
+    across, zy = lax.optimization_barrier((across, zy))
     twin_across = swap(across, bits[-1], n)
-    sk = third(f, m, tw, q_dev, tokens, A)
+    sk = third(fr, fi, zy, m, tw, q_dev, tokens, A)
     scores, t = score(lax.axis_index("store"), sk, [rows, across, twin, twin_across], bits, n)
     totals = jnp.sum(lax.all_to_all(t, "store", 0, 0), 0)
     return scores, totals / (n * q_dev)

time: 31.4 us -> 30.7 us (0.978)
  waiting for transfers between devices: 1.91 us -> 0.02 us
  starting transfers between devices: 7.83 us -> 9.17 us
    ppermute x0 -> x3, starting transfers between devices: none -> 7.01 us  [turn(): return lax.ppermute(v, 'store', [(i, (i + step) % n) for i in range(n)])]
    ppermute x6 -> x3, starting transfers between devices: 7.83 us -> 2.15 us  [swap(): return lax.ppermute(v, 'store', [(i, i ^ bit) for i in range(n)])]
    ppermute x6 -> x3, waiting for transfers between devices: 1.91 us -> 0.01 us  [swap(): return lax.ppermute(v, 'store', [(i, i ^ bit) for i in range(n)])]
  transfers between devices with their start and end apart: 6 -> 6, of which waited for: 1 -> 0; matrix products, arithmetic and copies ran while one was open for 0% -> 0% of each run, Pallas kernels for 29% -> 30%
where the time goes in v4:
time: 30.7 us; the launch traced here: 30.5 us
  Pallas kernels  10.3 us (34%)
  blocking collectives  9.68 us (32%)
  starting transfers between devices  9.17 us (30%)
  between operations  0.73 us (2%)
  other arithmetic  0.63 us (2%)
    all_to_all x1, blocking collectives, body(): totals = jnp.sum(lax.all_to_all(t, 'store', 0, 0), 0)  9.68 us
    pallas_call x3, Pallas kernels, call(): pl.pallas_call(kernel, out_shape=out, in_specs=[pl.BlockSpec(memory_space...  9.27 us
    ppermute x3, starting transfers between devices, turn(): return lax.ppermute(v, 'store', [(i, (i + step) % n) for i in range(n)])  7.01 us
    ppermute x3, starting transfers between devices, swap(): return lax.ppermute(v, 'store', [(i, i ^ bit) for i in range(n)])  2.15 us
    pallas_call x1, Pallas kernels, score(): pl.pallas_call(functools.partial(score_kernel, bits=bits, e=e, n=n), out_...  1 us
  transfers between devices with their start and end apart: 6, of which 0 were waited for; matrix products, arithmetic and copies ran while one was open for 0% of the time, Pallas kernels for 30%

profile of v4, /device:TPU:0, one launch (start us, length us, event | category | flops | bytes accessed | tf_op | source)
XLA Modules:
  0.0 30.5 jit_solution(2892077110083601699)
XLA Ops:
  0.6 3.1 %collective-permute-start = (bf16[4,4096]{1,0:T(4,128)(2,1)}, bf16[4,4096]{1,0:T(4,128)(2,1)S(1)}, u32[]{:S(2)}, u32[]{:S(2)}) collective-permute-start(bf16[4,4096]{1,0:T(4,128)(2,1)} %param.15), channel_id=1, source_target_pairs={{0,4},{1,5},{2,6},{3,7},{4,8},{5,9},{6,10},{7,11},{8,12},{9,13},{1... | collective-permute-start | bytes 98312 | tf_op jit(solution)/shard_map/ppermute | solution.py:271
  3.7 2.6 %collective-permute-start.1 = (bf16[4,4096]{1,0:T(4,128)(2,1)}, bf16[4,4096]{1,0:T(4,128)(2,1)S(1)}, u32[]{:S(2)}, u32[]{:S(2)}) collective-permute-start(bf16[4,4096]{1,0:T(4,128)(2,1)} %param.15), channel_id=1, source_target_pairs={{0,8},{1,9},{2,10},{3,11},{4,12},{5,13},{6,14},{7,15},{8,0},{9,1},... | collective-permute-start | bytes 98312 | tf_op jit(solution)/shard_map/ppermute | solution.py:271
  6.3 1.3 %collective-permute-start.2 = (bf16[4,4096]{1,0:T(4,128)(2,1)}, bf16[4,4096]{1,0:T(4,128)(2,1)S(1)}, u32[]{:S(2)}, u32[]{:S(2)}) collective-permute-start(bf16[4,4096]{1,0:T(4,128)(2,1)} %param.15), channel_id=1, source_target_pairs={{0,12},{1,13},{2,14},{3,15},{4,0},{5,1},{6,2},{7,3},{8,4},{9,5},{1... | collective-permute-start | bytes 98312 | tf_op jit(solution)/shard_map/ppermute | solution.py:271
  7.6 0.0 copy-start.2
  7.6 0.0 copy-start
  7.7 0.0 copy-start.1
  7.7 3.8 %shard_map.104 = (f32[1024,256]{1,0:T(8,128)S(1)}, bf16[64,4096]{1,0:T(8,128)(2,1)S(1)}, s32[32,128]{1,0:T(8,128)S(1)}, s32[32,128]{1,0:T(8,128)S(1)}) custom-call(s32[32,128]{1,0:T(8,128)} %bitcast.13, s32[32,128]{1,0:T(8,128)} %bitcast.14, bf16[64,4096]{1,0:T(8,128)(2,1)} %bitcast.11, s32[32,128]{1,0:T(8,128)} %bitcast.15, s32[32,128]{1,0:T(8,128)} %bitcast.16, ...), custom_call_target="tpu_custom_call" | custom-call | flops 2147483648 | bytes 4194304 | tf_op jit(solution)/shard_map/pallas_call | solution.py:177
  11.5 0.0 collective-permute-done
  11.5 0.0 collective-permute-done.1
  11.5 0.0 collective-permute-done.2
  11.5 0.0 copy-done.2
  11.5 0.1 pad_maximum_fusion.refs_0_
  11.6 1.6 %collective-permute-start.3 = (bf16[16,4096]{1,0:T(8,128)(2,1)S(1)}, bf16[16,4096]{1,0:T(8,128)(2,1)S(1)}, u32[]{:S(2)}, u32[]{:S(2)}) collective-permute-start(bf16[16,4096]{1,0:T(8,128)(2,1)S(1)} %pad_maximum_fusion.refs_0_), channel_id=1, source_target_pairs={{0,2},{1,3},{2,0},{3,1},{4,6},{5,7},{6,4},{7,5},{8,10},{9,11},{10,... | collective-permute-start | bytes 393224 | tf_op jit(solution)/shard_map/ppermute | solution.py:267
  13.2 0.0 collective-permute-start.4
  13.2 0.0 copy-done
  13.2 0.0 copy-done.1
  13.2 3.9 %shard_map.105 = (f32[576,256]{1,0:T(8,128)S(1)}, f32[576,256]{1,0:T(8,128)S(1)}, f32[576,512]{1,0:T(8,128)S(1)}) custom-call(f32[1024,256]{1,0:T(8,128)S(1)} %get-tuple-element.16.cx, bf16[64,4096]{1,0:T(8,128)(2,1)S(1)} %get-tuple-element.17.y, s32[32,128]{1,0:T(8,128)S(1)} %get-tuple-element.18.ho, s32[32,128]{1,0:T(8,128)S(1)} %get-tuple-element.19.so, ...), custom_call_target="tpu_custom_call" | custom-call | flops 2147483648 | bytes 4194304 | tf_op jit(solution)/shard_map/pallas_call | solution.py:177
  17.1 0.0 collective-permute-done.3.refs_1_
  17.1 0.6 %collective-permute-start.5 = (bf16[16,4096]{1,0:T(8,128)(2,1)S(1)}, bf16[16,4096]{1,0:T(8,128)(2,1)S(1)}, u32[]{:S(2)}, u32[]{:S(2)}) collective-permute-start(bf16[16,4096]{1,0:T(8,128)(2,1)S(1)} %collective-permute-done.3.refs_1_), channel_id=1, source_target_pairs={{0,1},{1,0},{2,3},{3,2},{4,5},{5,4},{6,7},{7,6},{8,9},{9,8},{10,11... | collective-permute-start | bytes 393224 | tf_op jit(solution)/shard_map/ppermute | solution.py:267
  17.7 1.6 %shard_map.106.sk_ref = bf16[4,4096]{1,0:T(4,128)(2,1)S(1)} custom-call(f32[576,256]{1,0:T(8,128)S(1)} %get-tuple-element.20.fr, f32[576,256]{1,0:T(8,128)S(1)} %get-tuple-element.21.fi, f32[576,512]{1,0:T(8,128)S(1)} %get-tuple-element.24.zy, bf16[1024,512]{1,0:T(8,128)(2,1)S(1)} %copy-done, f32[24,256]{1,0:T(8,128)S(1)} %copy-done.1), custom_call_target="tpu_custom_call" | custom-call | flops 2147483648 | bytes 4194304 | tf_op jit(solution)/shard_map/pallas_call | solution.py:177
  19.3 0.0 collective-permute-done.4.refs_2_
  19.3 0.0 collective-permute-done.5.refs_3_
  19.3 1.0 %shard_map.107 = (f32[4,64]{1,0:T(4,128)}, f32[16,4]{1,0:T(8,128)S(1)}) custom-call(s32[1]{0:T(128)} %bitcast.me_ref, bf16[4,4096]{1,0:T(4,128)(2,1)S(1)} %shard_map.106.sk_ref, bf16[16,4096]{1,0:T(8,128)(2,1)S(1)} %pad_maximum_fusion.refs_0_, bf16[16,4096]{1,0:T(8,128)(2,1)S(1)} %collective-permute-done.3.refs_1_, ...), custom_call_target="tpu_custom_call" | custom-call | flops 2097152 | bytes 524288 | tf_op jit(solution)/shard_map/pallas_call | solution.py:256
  20.3 9.7 %all_to_all.9 = f32[16,1,4]{2,1,0:T(1,128)S(1)} all-to-all(f32[16,1,4]{2,1,0:T(1,128)S(1)} %bitcast.10), channel_id=1, replica_groups=mesh['grp'=2,'store'=16] {'store'}, dimensions={0} | all-to-all | bytes 512 | tf_op jit(solution)/shard_map/all_to_all | solution.py:295
  30.0 0.5 %broadcast_multiply_fusion = f32[4]{0:T(128)} fusion(f32[4]{0:T(128)S(1)} %reduce_sum.9), kind=kLoop, calls=%fused_computation.1 | loop fusion | flops 4 | bytes 32 | tf_op jit(solution)/shard_map/div | solution.py:296
  (1 shorter events, 0.0 us)
Async XLA Ops:
  0.6 10.8 %collective-permute-start = (bf16[4,4096]{1,0:T(4,128)(2,1)}, bf16[4,4096]{1,0:T(4,128)(2,1)S(1)}, u32[]{:S(2)}, u32[]{:S(2)}) collective-permute-start(bf16[4,4096]{1,0:T(4,128)(2,1)} %param.15), channel_id=1, source_target_pairs={{0,4},{1,5},{2,6},{3,7},{4,8},{5,9},{6,10},{7,11},{8,12},{9,13},{1... | collective-permute-start | bytes 98312 | tf_op jit(solution)/shard_map/ppermute | solution.py:271
  3.7 7.8 %collective-permute-start.1 = (bf16[4,4096]{1,0:T(4,128)(2,1)}, bf16[4,4096]{1,0:T(4,128)(2,1)S(1)}, u32[]{:S(2)}, u32[]{:S(2)}) collective-permute-start(bf16[4,4096]{1,0:T(4,128)(2,1)} %param.15), channel_id=1, source_target_pairs={{0,8},{1,9},{2,10},{3,11},{4,12},{5,13},{6,14},{7,15},{8,0},{9,1},... | collective-permute-start | bytes 98312 | tf_op jit(solution)/shard_map/ppermute | solution.py:271
  6.3 5.2 %collective-permute-start.2 = (bf16[4,4096]{1,0:T(4,128)(2,1)}, bf16[4,4096]{1,0:T(4,128)(2,1)S(1)}, u32[]{:S(2)}, u32[]{:S(2)}) collective-permute-start(bf16[4,4096]{1,0:T(4,128)(2,1)} %param.15), channel_id=1, source_target_pairs={{0,12},{1,13},{2,14},{3,15},{4,0},{5,1},{6,2},{7,3},{8,4},{9,5},{1... | collective-permute-start | bytes 98312 | tf_op jit(solution)/shard_map/ppermute | solution.py:271
  7.6 3.8 %copy-start.2 = (bf16[4,4096]{1,0:T(4,128)(2,1)S(1)}, bf16[4,4096]{1,0:T(4,128)(2,1)}, u32[]{:S(2)}) copy-start(bf16[4,4096]{1,0:T(4,128)(2,1)} %param.15) | copy-start | bytes 98308
  7.6 5.5 %copy-start = (bf16[1024,512]{1,0:T(8,128)(2,1)S(1)}, bf16[1024,512]{1,0:T(8,128)(2,1)}, u32[]{:S(2)}) copy-start(bf16[1024,512]{1,0:T(8,128)(2,1)} %constant.13.clone.m) | copy-start | bytes 3145732
  7.7 5.5 %copy-start.1 = (f32[24,256]{1,0:T(8,128)S(1)}, f32[24,256]{1,0:T(8,128)}, u32[]{:S(2)}) copy-start(f32[24,256]{1,0:T(8,128)} %constant.14.clone.tw) | copy-start | bytes 73732
  11.6 5.5 %collective-permute-start.3 = (bf16[16,4096]{1,0:T(8,128)(2,1)S(1)}, bf16[16,4096]{1,0:T(8,128)(2,1)S(1)}, u32[]{:S(2)}, u32[]{:S(2)}) collective-permute-start(bf16[16,4096]{1,0:T(8,128)(2,1)S(1)} %pad_maximum_fusion.refs_0_), channel_id=1, source_target_pairs={{0,2},{1,3},{2,0},{3,1},{4,6},{5,7},{6,4},{7,5},{8,10},{9,11},{10,... | collective-permute-start | bytes 393224 | tf_op jit(solution)/shard_map/ppermute | solution.py:267
  13.2 6.1 %collective-permute-start.4 = (bf16[16,4096]{1,0:T(8,128)(2,1)S(1)}, bf16[16,4096]{1,0:T(8,128)(2,1)S(1)}, u32[]{:S(2)}, u32[]{:S(2)}) collective-permute-start(bf16[16,4096]{1,0:T(8,128)(2,1)S(1)} %pad_maximum_fusion.refs_0_), channel_id=1, source_target_pairs={{0,1},{1,0},{2,3},{3,2},{4,5},{5,4},{6,7},{7,6},{8,9},{9,8},{10,11... | collective-permute-start | bytes 393224 | tf_op jit(solution)/shard_map/ppermute | solution.py:267
  17.1 2.2 %collective-permute-start.5 = (bf16[16,4096]{1,0:T(8,128)(2,1)S(1)}, bf16[16,4096]{1,0:T(8,128)(2,1)S(1)}, u32[]{:S(2)}, u32[]{:S(2)}) collective-permute-start(bf16[16,4096]{1,0:T(8,128)(2,1)S(1)} %collective-permute-done.3.refs_1_), channel_id=1, source_target_pairs={{0,1},{1,0},{2,3},{3,2},{4,5},{5,4},{6,7},{7,6},{8,9},{9,8},{10,11... | collective-permute-start | bytes 393224 | tf_op jit(solution)/shard_map/ppermute | solution.py:267

commit v5 on v4

--- a/solution.py
+++ b/solution.py
@@ -115,23 +115,24 @@
     return out
 
 
-def first_kernel(*refs, A, W):
-    given, (cx, y, ho, so, x, hi, si, bt, sem) = refs[:6], refs[6:]
-    copies = [pltpu.make_async_copy(a, b, sem.at[i]) for i, (a, b) in enumerate(zip(given, (hi, si, x, ho, so, y)))]
+def first_kernel(*refs, Q, T, A, W):
+    given, (zx, y, ho, so, x, hi, si, tw, bt, cx, sem) = refs[:7], refs[7:]
+    copies = [pltpu.make_async_copy(a, b, sem.at[i]) for i, (a, b) in enumerate(zip(given, (hi, si, x, tw, ho, so, y)))]
     for c in copies:
         c.start()
-    for c in copies[:3]:
+    copies[0].wait()
+    onehot(hi, bt, W)
+    for c in copies[1:4]:
         c.wait()
-    onehot(hi, bt, W)
     cx[...] = count(x, hi, si, bt, A, W)
-    for c in copies[3:]:
+    for q in range(Q):
+        class_rows(cx, 0, Q * T, q, T, tw, zx, q * (A // 2 + 1) * T, A, W)
+    for c in copies[4:]:
         c.wait()
 
 
-def second_kernel(cx, y, ho, so, m, tw, fr, fi, zy, zx, cy, bt, *, Q, T, A, W):
+def second_kernel(zx, y, ho, so, m, tw, fr, fi, zy, cy, bt, *, Q, T, A, W):
     H, R = A // 2 + 1, Q * T
-    for q in range(Q):
-        class_rows(cx, 0, R, q, T, tw, zx, q * H * T, A, W)
     onehot(ho, bt, W)
     cy[...] = count(y, ho, so, bt, A, W)
     for q in range(Q):
@@ -185,22 +186,25 @@
     )(*args)
 
 
-def first(x, y, hi, si, ho, so, A, W):
-    R, D = x.shape
+def first(x, y, hi, si, ho, so, tw, A, Q):
+    (R, D), W = x.shape, tw.shape[1]
     like = lambda v: jax.ShapeDtypeStruct(v.shape, v.dtype)
-    args = [pltpu.with_memory_space_constraint(v, pltpu.HBM) for v in (hi, si, x, ho, so, y)]
-    scratch = [pltpu.VMEM(v.shape, v.dtype) for v in (x, hi, si)] + [pltpu.VMEM((W, D), bf), pltpu.SemaphoreType.DMA((6,))]
-    out = (jax.ShapeDtypeStruct((A * R, W), f32), like(y), like(ho), like(so))
-    return call(functools.partial(first_kernel, A=A, W=W), out, args, scratch, 2 * R * D * A * W, pltpu.HBM)
-
-
-def second(cx, y, ho, so, m, tw, Q, A):
-    W = cx.shape[1]
-    R = cx.shape[0] // A
-    rows = R * (A // 2 + 1)
-    out = (jax.ShapeDtypeStruct((rows, W), f32),) * 2 + (jax.ShapeDtypeStruct((rows, 2 * W), f32),)
-    scratch = [pltpu.VMEM((rows, 2 * W), f32), pltpu.VMEM(cx.shape, f32), pltpu.VMEM((W, y.shape[1]), bf)]
-    return call(functools.partial(second_kernel, Q=Q, T=R // Q, A=A, W=W), out, (cx, y, ho, so, m, tw), scratch, 2 * R * y.shape[1] * A * W)
+    args = [pltpu.with_memory_space_constraint(v, pltpu.HBM) for v in (hi, si, x, tw, ho, so, y)]
+    scratch = [pltpu.VMEM(v.shape, v.dtype) for v in (x, hi, si, tw)] + [pltpu.VMEM((W, D), bf), pltpu.VMEM((A * R, W), f32), pltpu.SemaphoreType.DMA((7,))]
+    out = (jax.ShapeDtypeStruct((R * (A // 2 + 1), 2 * W), f32), like(y), like(ho), like(so))
+    return call(functools.partial(first_kernel, Q=Q, T=R // Q, A=A, W=W), out, args, scratch, 2 * R * D * A * W, pltpu.HBM)
+
+
+def second(zx, y, ho, so, m, tw, Q, A):
+    rows, W = zx.shape[0], tw.shape[1]
+    R = rows // (A // 2 + 1)
+    out = (jax.ShapeDtypeStruct((rows, W), f32),) * 2 + (like_rows(rows, W),)
+    scratch = [pltpu.VMEM((A * R, W), f32), pltpu.VMEM((W, y.shape[1]), bf)]
+    return call(functools.partial(second_kernel, Q=Q, T=R // Q, A=A, W=W), out, (zx, y, ho, so, m, tw), scratch, 2 * R * y.shape[1] * A * W)
+
+
+def like_rows(rows, W):
+    return jax.ShapeDtypeStruct((rows, 2 * W), f32)
 
 
 def third(fr, fi, zy, m, tw, Q, R, A):
@@ -281,13 +285,13 @@
     m, tw = (jnp.asarray(v) for v in tables(A, width // A))
     tokens = q_dev * query_inputs.shape[1]
     tabs = (v.reshape(-1, 128) for v in (hash_in, sign_in, hash_out, sign_out))
-    cx, *rest = first(query_inputs.reshape(tokens, -1), query_grads.reshape(tokens, -1), *tabs, A, width // A)
-    rows, cx = lax.optimization_barrier((jnp.concatenate(parts, 0), cx))
+    zx, *rest = first(query_inputs.reshape(tokens, -1), query_grads.reshape(tokens, -1), *tabs, tw, A, q_dev)
+    rows, zx = lax.optimization_barrier((jnp.concatenate(parts, 0), zx))
     for bit in bits[2:-2]:
         rows = jnp.concatenate([rows, swap(rows, bit, n)], 0)
     across = swap(rows, bits[-2], n)
     twin = swap(rows, bits[-1], n)
-    fr, fi, zy = second(cx, *rest, m, tw, q_dev, A)
+    fr, fi, zy = second(zx, *rest, m, tw, q_dev, A)
     across, zy = lax.optimization_barrier((across, zy))
     twin_across = swap(across, bits[-1], n)
     sk = third(fr, fi, zy, m, tw, q_dev, tokens, A)

time: 30.7 us -> 30.7 us (level)
  transfers between devices with their start and end apart: 6 -> 6, of which waited for: 0 -> 0; matrix products, arithmetic and copies ran while one was open for 0% -> 0% of each run, Pallas kernels for 30% -> 31%
where the time goes in v5:
time: 30.7 us; the launch traced here: 30.5 us
  Pallas kernels  10.3 us (34%)
  blocking collectives  9.61 us (31%)
  starting transfers between devices  9.17 us (30%)
  between operations  0.73 us (2%)
  other arithmetic  0.63 us (2%)
    all_to_all x1, blocking collectives, body(): totals = jnp.sum(lax.all_to_all(t, 'store', 0, 0), 0)  9.61 us
    pallas_call x3, Pallas kernels, call(): pl.pallas_call(kernel, out_shape=out, in_specs=[pl.BlockSpec(memory_space...  9.34 us
    ppermute x3, starting transfers between devices, turn(): return lax.ppermute(v, 'store', [(i, (i + step) % n) for i in range(n)])  7.01 us
    ppermute x3, starting transfers between devices, swap(): return lax.ppermute(v, 'store', [(i, i ^ bit) for i in range(n)])  2.16 us
    pallas_call x1, Pallas kernels, score(): pl.pallas_call(functools.partial(score_kernel, bits=bits, e=e, n=n), out_...  1 us
  transfers between devices with their start and end apart: 6, of which 0 were waited for; matrix products, arithmetic and copies ran while one was open for 0% of the time, Pallas kernels for 31%

profile of v5, /device:TPU:0, one launch (start us, length us, event | category | flops | bytes accessed | tf_op | source)
XLA Modules:
  0.0 30.5 jit_solution(127420317595203040)
XLA Ops:
  0.6 3.1 %collective-permute-start = (bf16[4,4096]{1,0:T(4,128)(2,1)}, bf16[4,4096]{1,0:T(4,128)(2,1)S(1)}, u32[]{:S(2)}, u32[]{:S(2)}) collective-permute-start(bf16[4,4096]{1,0:T(4,128)(2,1)} %param.15), channel_id=1, source_target_pairs={{0,4},{1,5},{2,6},{3,7},{4,8},{5,9},{6,10},{7,11},{8,12},{9,13},{1... | collective-permute-start | bytes 98312 | tf_op jit(solution)/shard_map/ppermute | solution.py:275
  3.7 2.6 %collective-permute-start.1 = (bf16[4,4096]{1,0:T(4,128)(2,1)}, bf16[4,4096]{1,0:T(4,128)(2,1)S(1)}, u32[]{:S(2)}, u32[]{:S(2)}) collective-permute-start(bf16[4,4096]{1,0:T(4,128)(2,1)} %param.15), channel_id=1, source_target_pairs={{0,8},{1,9},{2,10},{3,11},{4,12},{5,13},{6,14},{7,15},{8,0},{9,1},... | collective-permute-start | bytes 98312 | tf_op jit(solution)/shard_map/ppermute | solution.py:275
  6.3 1.3 %collective-permute-start.2 = (bf16[4,4096]{1,0:T(4,128)(2,1)}, bf16[4,4096]{1,0:T(4,128)(2,1)S(1)}, u32[]{:S(2)}, u32[]{:S(2)}) collective-permute-start(bf16[4,4096]{1,0:T(4,128)(2,1)} %param.15), channel_id=1, source_target_pairs={{0,12},{1,13},{2,14},{3,15},{4,0},{5,1},{6,2},{7,3},{8,4},{9,5},{1... | collective-permute-start | bytes 98312 | tf_op jit(solution)/shard_map/ppermute | solution.py:275
  7.6 0.0 copy-start.2
  7.6 0.0 copy-start
  7.7 0.0 copy-start.1
  7.7 4.0 %shard_map.104 = (f32[576,512]{1,0:T(8,128)S(1)}, bf16[64,4096]{1,0:T(8,128)(2,1)S(1)}, s32[32,128]{1,0:T(8,128)S(1)}, s32[32,128]{1,0:T(8,128)S(1)}) custom-call(s32[32,128]{1,0:T(8,128)} %bitcast.13, s32[32,128]{1,0:T(8,128)} %bitcast.14, bf16[64,4096]{1,0:T(8,128)(2,1)} %bitcast.11, f32[24,256]{1,0:T(8,128)} %constant.14.clone.refs_3_.tw, ...), custom_call_target="tpu_custom_call" | custom-call | flops 2147483648 | bytes 4194304 | tf_op jit(solution)/shard_map/pallas_call | solution.py:178
  11.6 0.0 collective-permute-done
  11.7 0.0 collective-permute-done.1
  11.7 0.0 collective-permute-done.2
  11.7 0.0 copy-done.2
  11.7 0.1 pad_maximum_fusion.refs_0_
  11.8 1.6 %collective-permute-start.3 = (bf16[16,4096]{1,0:T(8,128)(2,1)S(1)}, bf16[16,4096]{1,0:T(8,128)(2,1)S(1)}, u32[]{:S(2)}, u32[]{:S(2)}) collective-permute-start(bf16[16,4096]{1,0:T(8,128)(2,1)S(1)} %pad_maximum_fusion.refs_0_), channel_id=1, source_target_pairs={{0,2},{1,3},{2,0},{3,1},{4,6},{5,7},{6,4},{7,5},{8,10},{9,11},{10,... | collective-permute-start | bytes 393224 | tf_op jit(solution)/shard_map/ppermute | solution.py:271
  13.4 0.0 collective-permute-start.4
  13.4 0.0 copy-done
  13.4 0.0 copy-done.1
  13.4 3.8 %shard_map.105 = (f32[576,256]{1,0:T(8,128)S(1)}, f32[576,256]{1,0:T(8,128)S(1)}, f32[576,512]{1,0:T(8,128)S(1)}) custom-call(f32[576,512]{1,0:T(8,128)S(1)} %get-tuple-element.16.zx, bf16[64,4096]{1,0:T(8,128)(2,1)S(1)} %get-tuple-element.17.y, s32[32,128]{1,0:T(8,128)S(1)} %get-tuple-element.18.ho, s32[32,128]{1,0:T(8,128)S(1)} %get-tuple-element.19.so, ...), custom_call_target="tpu_custom_call" | custom-call | flops 2147483648 | bytes 4194304 | tf_op jit(solution)/shard_map/pallas_call | solution.py:178
  17.1 0.0 collective-permute-done.3.refs_1_
  17.2 0.6 %collective-permute-start.5 = (bf16[16,4096]{1,0:T(8,128)(2,1)S(1)}, bf16[16,4096]{1,0:T(8,128)(2,1)S(1)}, u32[]{:S(2)}, u32[]{:S(2)}) collective-permute-start(bf16[16,4096]{1,0:T(8,128)(2,1)S(1)} %collective-permute-done.3.refs_1_), channel_id=1, source_target_pairs={{0,1},{1,0},{2,3},{3,2},{4,5},{5,4},{6,7},{7,6},{8,9},{9,8},{10,11... | collective-permute-start | bytes 393224 | tf_op jit(solution)/shard_map/ppermute | solution.py:271
  17.7 1.6 %shard_map.106.sk_ref = bf16[4,4096]{1,0:T(4,128)(2,1)S(1)} custom-call(f32[576,256]{1,0:T(8,128)S(1)} %get-tuple-element.20.fr, f32[576,256]{1,0:T(8,128)S(1)} %get-tuple-element.21.fi, f32[576,512]{1,0:T(8,128)S(1)} %get-tuple-element.24.zy, bf16[1024,512]{1,0:T(8,128)(2,1)S(1)} %copy-done, f32[24,256]{1,0:T(8,128)S(1)} %copy-done.1), custom_call_target="tpu_custom_call" | custom-call | flops 2147483648 | bytes 4194304 | tf_op jit(solution)/shard_map/pallas_call | solution.py:178
  19.3 0.0 collective-permute-done.4.refs_2_
  19.3 0.0 collective-permute-done.5.refs_3_
  19.4 1.0 %shard_map.107 = (f32[4,64]{1,0:T(4,128)}, f32[16,4]{1,0:T(8,128)S(1)}) custom-call(s32[1]{0:T(128)} %bitcast.me_ref, bf16[4,4096]{1,0:T(4,128)(2,1)S(1)} %shard_map.106.sk_ref, bf16[16,4096]{1,0:T(8,128)(2,1)S(1)} %pad_maximum_fusion.refs_0_, bf16[16,4096]{1,0:T(8,128)(2,1)S(1)} %collective-permute-done.3.refs_1_, ...), custom_call_target="tpu_custom_call" | custom-call | flops 2097152 | bytes 524288 | tf_op jit(solution)/shard_map/pallas_call | solution.py:260
  20.4 9.6 %all_to_all.9 = f32[16,1,4]{2,1,0:T(1,128)S(1)} all-to-all(f32[16,1,4]{2,1,0:T(1,128)S(1)} %bitcast.10), channel_id=1, replica_groups=mesh['grp'=2,'store'=16] {'store'}, dimensions={0} | all-to-all | bytes 512 | tf_op jit(solution)/shard_map/all_to_all | solution.py:299
  30.0 0.5 %broadcast_multiply_fusion = f32[4]{0:T(128)} fusion(f32[4]{0:T(128)S(1)} %reduce_sum.9), kind=kLoop, calls=%fused_computation.1 | loop fusion | flops 4 | bytes 32 | tf_op jit(solution)/shard_map/div | solution.py:300
  (1 shorter events, 0.0 us)
Async XLA Ops:
  0.6 11.0 %collective-permute-start = (bf16[4,4096]{1,0:T(4,128)(2,1)}, bf16[4,4096]{1,0:T(4,128)(2,1)S(1)}, u32[]{:S(2)}, u32[]{:S(2)}) collective-permute-start(bf16[4,4096]{1,0:T(4,128)(2,1)} %param.15), channel_id=1, source_target_pairs={{0,4},{1,5},{2,6},{3,7},{4,8},{5,9},{6,10},{7,11},{8,12},{9,13},{1... | collective-permute-start | bytes 98312 | tf_op jit(solution)/shard_map/ppermute | solution.py:275
  3.7 8.0 %collective-permute-start.1 = (bf16[4,4096]{1,0:T(4,128)(2,1)}, bf16[4,4096]{1,0:T(4,128)(2,1)S(1)}, u32[]{:S(2)}, u32[]{:S(2)}) collective-permute-start(bf16[4,4096]{1,0:T(4,128)(2,1)} %param.15), channel_id=1, source_target_pairs={{0,8},{1,9},{2,10},{3,11},{4,12},{5,13},{6,14},{7,15},{8,0},{9,1},... | collective-permute-start | bytes 98312 | tf_op jit(solution)/shard_map/ppermute | solution.py:275
  6.3 5.4 %collective-permute-start.2 = (bf16[4,4096]{1,0:T(4,128)(2,1)}, bf16[4,4096]{1,0:T(4,128)(2,1)S(1)}, u32[]{:S(2)}, u32[]{:S(2)}) collective-permute-start(bf16[4,4096]{1,0:T(4,128)(2,1)} %param.15), channel_id=1, source_target_pairs={{0,12},{1,13},{2,14},{3,15},{4,0},{5,1},{6,2},{7,3},{8,4},{9,5},{1... | collective-permute-start | bytes 98312 | tf_op jit(solution)/shard_map/ppermute | solution.py:275
  7.6 4.0 %copy-start.2 = (bf16[4,4096]{1,0:T(4,128)(2,1)S(1)}, bf16[4,4096]{1,0:T(4,128)(2,1)}, u32[]{:S(2)}) copy-start(bf16[4,4096]{1,0:T(4,128)(2,1)} %param.15) | copy-start | bytes 98308
  7.6 5.7 %copy-start = (bf16[1024,512]{1,0:T(8,128)(2,1)S(1)}, bf16[1024,512]{1,0:T(8,128)(2,1)}, u32[]{:S(2)}) copy-start(bf16[1024,512]{1,0:T(8,128)(2,1)} %constant.13.clone.m) | copy-start | bytes 3145732
  7.7 5.7 %copy-start.1 = (f32[24,256]{1,0:T(8,128)S(1)}, f32[24,256]{1,0:T(8,128)}, u32[]{:S(2)}) copy-start(f32[24,256]{1,0:T(8,128)} %constant.14.clone.refs_3_.tw) | copy-start | bytes 73732
  11.8 5.4 %collective-permute-start.3 = (bf16[16,4096]{1,0:T(8,128)(2,1)S(1)}, bf16[16,4096]{1,0:T(8,128)(2,1)S(1)}, u32[]{:S(2)}, u32[]{:S(2)}) collective-permute-start(bf16[16,4096]{1,0:T(8,128)(2,1)S(1)} %pad_maximum_fusion.refs_0_), channel_id=1, source_target_pairs={{0,2},{1,3},{2,0},{3,1},{4,6},{5,7},{6,4},{7,5},{8,10},{9,11},{10,... | collective-permute-start | bytes 393224 | tf_op jit(solution)/shard_map/ppermute | solution.py:271
  13.4 6.0 %collective-permute-start.4 = (bf16[16,4096]{1,0:T(8,128)(2,1)S(1)}, bf16[16,4096]{1,0:T(8,128)(2,1)S(1)}, u32[]{:S(2)}, u32[]{:S(2)}) collective-permute-start(bf16[16,4096]{1,0:T(8,128)(2,1)S(1)} %pad_maximum_fusion.refs_0_), channel_id=1, source_target_pairs={{0,1},{1,0},{2,3},{3,2},{4,5},{5,4},{6,7},{7,6},{8,9},{9,8},{10,11... | collective-permute-start | bytes 393224 | tf_op jit(solution)/shard_map/ppermute | solution.py:271
  17.2 2.2 %collective-permute-start.5 = (bf16[16,4096]{1,0:T(8,128)(2,1)S(1)}, bf16[16,4096]{1,0:T(8,128)(2,1)S(1)}, u32[]{:S(2)}, u32[]{:S(2)}) collective-permute-start(bf16[16,4096]{1,0:T(8,128)(2,1)S(1)} %collective-permute-done.3.refs_1_), channel_id=1, source_target_pairs={{0,1},{1,0},{2,3},{3,2},{4,5},{5,4},{6,7},{7,6},{8,9},{9,8},{10,11... | collective-permute-start | bytes 393224 | tf_op jit(solution)/shard_map/ppermute | solution.py:271
